TPU v7x, 1024 devices: a whole 4x4x32 slice. The times are simulated.
1024 devices in a mesh: row: 16 (over x, y), col: 16 (over z_lo), layer: 4 (over z_hi, core).
Axes of the slice: x: 4, y: 4, z: 32 (z_hi: 2, z_lo: 16; z = z_hi * 16 + z_lo), core: 2. Of those that a mesh axis runs over, the one named last changes fastest.
Arguments:
- slab: bfloat16 [7360, 11776], P(('layer', 'row'), 'col'), may hold values from -6 to 6
- green: bfloat16 [7360, 8832], P(('layer', 'col'), 'row'), may hold values from -0.375 to 0.375
- mask_slab: int32 [320, 512], P(('layer', 'row'), 'col'), may hold values from 0 to 1, as said below
- mask_green: int32 [320, 384], P(('layer', 'col'), 'row'), may hold values from 0 to 1, as said below
Outputs:
- product: bfloat16 [11776, 8832], P('col', ('row', 'layer'))
Inputs may be any that keep to these rules, and one draw needn't show every extreme that they name: `mask_slab`: 0 or 1 per atom block. Each device's piece of 5 x 32 atom blocks holds at least one and at most 40 live blocks; some piece holds exactly 40. `mask_green`: 0 or 1 per atom block. Each device's piece of 5 x 24 atom blocks holds at least one and at most 30 live blocks; some piece holds exactly 30.
All inputs are finite; a program needn't handle non-finite values.
Results may differ from a plain program's by a relative error of at most 0.001.
Values may be sent and summed in bfloat16 or wider, within the bound.
A program may use at most 32 MiB of HBM per device.

v0:
```python
import jax
import jax.numpy as jnp
from jax import lax
from jax.sharding import PartitionSpec as P

BLK = 23


def passed_along(shard, axis, by):
    count = lax.axis_size(axis)
    return lax.ppermute(shard, axis, [(i, (i + by) % count) for i in range(count)])


def expand(mask):
    return jnp.repeat(jnp.repeat(mask, BLK, axis=0), BLK, axis=1).astype(jnp.bfloat16)


def contract(left, right):
    return lax.dot_general(
        left, right, (((0,), (0,)), ((), ())), preferred_element_type=jnp.float32
    )


def shards(slab, green, mask_slab, mask_green):
    slab_live = slab * expand(mask_slab)
    green_live = green * expand(mask_green)
    rounds = lax.axis_size("row")
    total = jnp.zeros((slab.shape[1], green.shape[1]), jnp.float32)
    grid_row = lax.axis_index("row")
    grid_col = lax.axis_index("col")
    for bit in range(rounds.bit_length() - 1):
        moved = passed_along(slab_live, "row", -(1 << bit))
        slab_live = jnp.where(grid_col >> bit & 1 == 1, moved, slab_live)
    for bit in range(rounds.bit_length() - 1):
        moved = passed_along(green_live, "col", -(1 << bit))
        green_live = jnp.where(grid_row >> bit & 1 == 1, moved, green_live)

    def advance(turn, carry):
        left, right, acc = carry
        next_left = passed_along(left, "row", -1)
        next_right = passed_along(right, "col", -1)
        return (next_left, next_right, acc + contract(left, right))

    left, right, total = lax.fori_loop(0, rounds - 1, advance, (slab_live, green_live, total))
    total = total + contract(left, right)
    shared = lax.psum_scatter(total, "layer", scatter_dimension=1, tiled=True)
    return shared.astype(jnp.bfloat16)


def solution(mesh):
    in_specs = (
        P(("layer", "row"), "col"),
        P(("layer", "col"), "row"),
        P(("layer", "row"), "col"),
        P(("layer", "col"), "row"),
    )
    out_specs = P("col", ("row", "layer"))
    return jax.shard_map(shards, mesh=mesh, in_specs=in_specs, out_specs=out_specs, check_vma=False)
```

profile of v0, /device:TPU:1, one launch (start us, length us, event | category | flops | bytes accessed | tf_op | source)
XLA Modules:
  0.0 594.9 jit_solution(6538303108483373145)
XLA Ops:
  0.0 0.7 convert_element_type.28
  1.1 1.0 mul.7
  2.1 27.0 %collective-permute-start.6 = (bf16[115,552]{0,1:T(8,128)(2,1)S(1)}, bf16[115,552]{0,1:T(8,128)(2,1)S(1)}, u32[]{:S(2)}, u32[]{:S(2)}) collective-permute-start(bf16[115,552]{0,1:T(8,128)(2,1)S(1)} %mul.7), channel_id=1, source_target_pairs={{0,60},{4,0},{8,4},{12,8},{16,12},{20,16},{24,20},{28,24},{32,28},... | collective-permute-start | bytes 380888 | tf_op jit(solution)/shard_map/ppermute | solution.py:11
  30.2 6.8 %collective-permute-start.2 = (bf16[115,736]{0,1:T(8,128)(2,1)S(1)}, bf16[115,736]{0,1:T(8,128)(2,1)S(1)}, u32[]{:S(2)}, u32[]{:S(2)}) collective-permute-start(bf16[115,736]{0,1:T(8,128)(2,1)S(1)} %mul.6), channel_id=1, source_target_pairs={{0,960},{64,0},{128,64},{192,128},{256,192},{320,256},{384,320},{4... | collective-permute-start | bytes 507848 | tf_op jit(solution)/shard_map/ppermute | solution.py:11
  37.1 1.9 collective-permute-start.7
  39.1 1.0 collective-permute-done.2
  40.1 4.3 collective-permute-start.3
  44.5 1.9 collective-permute-start.8
  46.4 1.5 collective-permute-done.3
  48.0 2.5 collective-permute-start.4
  50.5 7.1 %collective-permute-done.8 = bf16[115,552]{0,1:T(8,128)(2,1)S(1)} collective-permute-done((bf16[115,552]{0,1:T(8,128)(2,1)S(1)}, bf16[115,552]{0,1:T(8,128)(2,1)S(1)}, u32[]{:S(2)}, u32[]{:S(2)}) %collective-permute-start.8) | collective-permute-done | bytes 126992 | tf_op jit(solution)/shard_map/ppermute | solution.py:11
  57.6 1.9 collective-permute-start.9
  59.6 3.1 collective-permute-start.5
  62.6 13.2 %collective-permute-done.9 = bf16[115,552]{0,1:T(8,128)(2,1)S(1)} collective-permute-done((bf16[115,552]{0,1:T(8,128)(2,1)S(1)}, bf16[115,552]{0,1:T(8,128)(2,1)S(1)}, u32[]{:S(2)}, u32[]{:S(2)}) %collective-permute-start.9) | collective-permute-done | bytes 126992 | tf_op jit(solution)/shard_map/ppermute | solution.py:11
  76.3 415.7 %while.15 = (s32[]{:T(128)}, bf16[115,736]{1,0:T(8,128)(2,1)S(1)}, bf16[115,552]{1,0:T(8,128)(2,1)S(1)}, f32[736,552]{0,1:T(8,128)S(1)}, s32[]{:T(128)}, /*index=5*/s32[]{:T(128)}) while((s32[]{:T(128)}, bf16[115,736]{1,0:T(8,128)(2,1)S(1)}, bf16[115,552]{1,0:T(8,128)(2,1)S(1)}, f32[736,552]{0,1:T(8,128)S(1)}, s32[]{:T(128)}, ...), condition=%wide.region_1.2_spmd.clone, body=%wide.region_0.1_spmd.clone.sunk | while | flops 94255104 | bytes 5324015 | solution.py:44
  76.3 4.3 collective-permute-start
  80.6 34.9 %collective-permute-start.1 = (bf16[115,552]{1,0:T(8,128)(2,1)S(1)}, bf16[115,552]{1,0:T(8,128)(2,1)S(1)}, u32[]{:S(2)}, u32[]{:S(2)}) collective-permute-start(bf16[115,552]{1,0:T(8,128)(2,1)S(1)} %copy.22), channel_id=1, source_target_pairs={{0,60},{4,0},{8,4},{12,8},{16,12},{20,16},{24,20},{28,24},{32,28},... | collective-permute-start | bytes 380888 | tf_op jit(solution)/shard_map/while/body/eval_jaxpr/ppermute | solution.py:11
  116.2 1.5 collective-permute-done.1
  117.7 6.9 %collective-permute-start = (bf16[115,736]{1,0:T(8,128)(2,1)S(1)}, bf16[115,736]{1,0:T(8,128)(2,1)S(1)}, u32[]{:S(2)}, u32[]{:S(2)}) collective-permute-start(bf16[115,736]{1,0:T(8,128)(2,1)S(1)} %copy.21), channel_id=1, source_target_pairs={{0,960},{64,0},{128,64},{192,128},{256,192},{320,256},{384,320},{4... | collective-permute-start | bytes 507848 | tf_op jit(solution)/shard_map/while/body/eval_jaxpr/ppermute | solution.py:11
  124.7 20.0 %collective-permute-start.1 = (bf16[115,552]{1,0:T(8,128)(2,1)S(1)}, bf16[115,552]{1,0:T(8,128)(2,1)S(1)}, u32[]{:S(2)}, u32[]{:S(2)}) collective-permute-start(bf16[115,552]{1,0:T(8,128)(2,1)S(1)} %copy.22), channel_id=1, source_target_pairs={{0,60},{4,0},{8,4},{12,8},{16,12},{20,16},{24,20},{28,24},{32,28},... | collective-permute-start | bytes 380888 | tf_op jit(solution)/shard_map/while/body/eval_jaxpr/ppermute | solution.py:11
  145.4 1.5 collective-permute-done.1
  146.9 1.9 collective-permute-start
  148.8 20.0 %collective-permute-start.1 = (bf16[115,552]{1,0:T(8,128)(2,1)S(1)}, bf16[115,552]{1,0:T(8,128)(2,1)S(1)}, u32[]{:S(2)}, u32[]{:S(2)}) collective-permute-start(bf16[115,552]{1,0:T(8,128)(2,1)S(1)} %copy.22), channel_id=1, source_target_pairs={{0,60},{4,0},{8,4},{12,8},{16,12},{20,16},{24,20},{28,24},{32,28},... | collective-permute-start | bytes 380888 | tf_op jit(solution)/shard_map/while/body/eval_jaxpr/ppermute | solution.py:11
  169.5 1.5 collective-permute-done.1
  171.0 1.9 collective-permute-start
  173.0 20.0 %collective-permute-start.1 = (bf16[115,552]{1,0:T(8,128)(2,1)S(1)}, bf16[115,552]{1,0:T(8,128)(2,1)S(1)}, u32[]{:S(2)}, u32[]{:S(2)}) collective-permute-start(bf16[115,552]{1,0:T(8,128)(2,1)S(1)} %copy.22), channel_id=1, source_target_pairs={{0,60},{4,0},{8,4},{12,8},{16,12},{20,16},{24,20},{28,24},{32,28},... | collective-permute-start | bytes 380888 | tf_op jit(solution)/shard_map/while/body/eval_jaxpr/ppermute | solution.py:11
  193.7 1.5 collective-permute-done.1
  195.2 1.9 collective-permute-start
  197.1 20.0 %collective-permute-start.1 = (bf16[115,552]{1,0:T(8,128)(2,1)S(1)}, bf16[115,552]{1,0:T(8,128)(2,1)S(1)}, u32[]{:S(2)}, u32[]{:S(2)}) collective-permute-start(bf16[115,552]{1,0:T(8,128)(2,1)S(1)} %copy.22), channel_id=1, source_target_pairs={{0,60},{4,0},{8,4},{12,8},{16,12},{20,16},{24,20},{28,24},{32,28},... | collective-permute-start | bytes 380888 | tf_op jit(solution)/shard_map/while/body/eval_jaxpr/ppermute | solution.py:11
  217.8 1.5 collective-permute-done.1
  219.3 6.4 %collective-permute-start = (bf16[115,736]{1,0:T(8,128)(2,1)S(1)}, bf16[115,736]{1,0:T(8,128)(2,1)S(1)}, u32[]{:S(2)}, u32[]{:S(2)}) collective-permute-start(bf16[115,736]{1,0:T(8,128)(2,1)S(1)} %copy.21), channel_id=1, source_target_pairs={{0,960},{64,0},{128,64},{192,128},{256,192},{320,256},{384,320},{4... | collective-permute-start | bytes 507848 | tf_op jit(solution)/shard_map/while/body/eval_jaxpr/ppermute | solution.py:11
  225.7 20.0 %collective-permute-start.1 = (bf16[115,552]{1,0:T(8,128)(2,1)S(1)}, bf16[115,552]{1,0:T(8,128)(2,1)S(1)}, u32[]{:S(2)}, u32[]{:S(2)}) collective-permute-start(bf16[115,552]{1,0:T(8,128)(2,1)S(1)} %copy.22), channel_id=1, source_target_pairs={{0,60},{4,0},{8,4},{12,8},{16,12},{20,16},{24,20},{28,24},{32,28},... | collective-permute-start | bytes 380888 | tf_op jit(solution)/shard_map/while/body/eval_jaxpr/ppermute | solution.py:11
  246.4 1.5 collective-permute-done.1
  247.9 1.9 collective-permute-start
  249.8 20.0 %collective-permute-start.1 = (bf16[115,552]{1,0:T(8,128)(2,1)S(1)}, bf16[115,552]{1,0:T(8,128)(2,1)S(1)}, u32[]{:S(2)}, u32[]{:S(2)}) collective-permute-start(bf16[115,552]{1,0:T(8,128)(2,1)S(1)} %copy.22), channel_id=1, source_target_pairs={{0,60},{4,0},{8,4},{12,8},{16,12},{20,16},{24,20},{28,24},{32,28},... | collective-permute-start | bytes 380888 | tf_op jit(solution)/shard_map/while/body/eval_jaxpr/ppermute | solution.py:11
  270.5 1.5 collective-permute-done.1
  272.0 1.9 collective-permute-start
  274.0 20.0 %collective-permute-start.1 = (bf16[115,552]{1,0:T(8,128)(2,1)S(1)}, bf16[115,552]{1,0:T(8,128)(2,1)S(1)}, u32[]{:S(2)}, u32[]{:S(2)}) collective-permute-start(bf16[115,552]{1,0:T(8,128)(2,1)S(1)} %copy.22), channel_id=1, source_target_pairs={{0,60},{4,0},{8,4},{12,8},{16,12},{20,16},{24,20},{28,24},{32,28},... | collective-permute-start | bytes 380888 | tf_op jit(solution)/shard_map/while/body/eval_jaxpr/ppermute | solution.py:11
  294.7 1.5 collective-permute-done.1
  296.2 1.9 collective-permute-start
  298.1 20.0 %collective-permute-start.1 = (bf16[115,552]{1,0:T(8,128)(2,1)S(1)}, bf16[115,552]{1,0:T(8,128)(2,1)S(1)}, u32[]{:S(2)}, u32[]{:S(2)}) collective-permute-start(bf16[115,552]{1,0:T(8,128)(2,1)S(1)} %copy.22), channel_id=1, source_target_pairs={{0,60},{4,0},{8,4},{12,8},{16,12},{20,16},{24,20},{28,24},{32,28},... | collective-permute-start | bytes 380888 | tf_op jit(solution)/shard_map/while/body/eval_jaxpr/ppermute | solution.py:11
  318.8 1.5 collective-permute-done.1
  320.3 5.3 collective-permute-start
  325.7 20.0 %collective-permute-start.1 = (bf16[115,552]{1,0:T(8,128)(2,1)S(1)}, bf16[115,552]{1,0:T(8,128)(2,1)S(1)}, u32[]{:S(2)}, u32[]{:S(2)}) collective-permute-start(bf16[115,552]{1,0:T(8,128)(2,1)S(1)} %copy.22), channel_id=1, source_target_pairs={{0,60},{4,0},{8,4},{12,8},{16,12},{20,16},{24,20},{28,24},{32,28},... | collective-permute-start | bytes 380888 | tf_op jit(solution)/shard_map/while/body/eval_jaxpr/ppermute | solution.py:11
  346.4 1.5 collective-permute-done.1
  347.9 1.9 collective-permute-start
  349.8 20.0 %collective-permute-start.1 = (bf16[115,552]{1,0:T(8,128)(2,1)S(1)}, bf16[115,552]{1,0:T(8,128)(2,1)S(1)}, u32[]{:S(2)}, u32[]{:S(2)}) collective-permute-start(bf16[115,552]{1,0:T(8,128)(2,1)S(1)} %copy.22), channel_id=1, source_target_pairs={{0,60},{4,0},{8,4},{12,8},{16,12},{20,16},{24,20},{28,24},{32,28},... | collective-permute-start | bytes 380888 | tf_op jit(solution)/shard_map/while/body/eval_jaxpr/ppermute | solution.py:11
  370.5 1.5 collective-permute-done.1
  372.0 1.9 collective-permute-start
  374.0 20.0 %collective-permute-start.1 = (bf16[115,552]{1,0:T(8,128)(2,1)S(1)}, bf16[115,552]{1,0:T(8,128)(2,1)S(1)}, u32[]{:S(2)}, u32[]{:S(2)}) collective-permute-start(bf16[115,552]{1,0:T(8,128)(2,1)S(1)} %copy.22), channel_id=1, source_target_pairs={{0,60},{4,0},{8,4},{12,8},{16,12},{20,16},{24,20},{28,24},{32,28},... | collective-permute-start | bytes 380888 | tf_op jit(solution)/shard_map/while/body/eval_jaxpr/ppermute | solution.py:11
  394.7 1.5 collective-permute-done.1
  396.2 1.9 collective-permute-start
  398.1 20.1 %collective-permute-start.1 = (bf16[115,552]{1,0:T(8,128)(2,1)S(1)}, bf16[115,552]{1,0:T(8,128)(2,1)S(1)}, u32[]{:S(2)}, u32[]{:S(2)}) collective-permute-start(bf16[115,552]{1,0:T(8,128)(2,1)S(1)} %copy.22), channel_id=1, source_target_pairs={{0,60},{4,0},{8,4},{12,8},{16,12},{20,16},{24,20},{28,24},{32,28},... | collective-permute-start | bytes 380888 | tf_op jit(solution)/shard_map/while/body/eval_jaxpr/ppermute | solution.py:11
  418.9 2.9 collective-permute-done.1
  421.8 2.4 collective-permute-start
  424.2 20.1 %collective-permute-start.1 = (bf16[115,552]{1,0:T(8,128)(2,1)S(1)}, bf16[115,552]{1,0:T(8,128)(2,1)S(1)}, u32[]{:S(2)}, u32[]{:S(2)}) collective-permute-start(bf16[115,552]{1,0:T(8,128)(2,1)S(1)} %copy.22), channel_id=1, source_target_pairs={{0,60},{4,0},{8,4},{12,8},{16,12},{20,16},{24,20},{28,24},{32,28},... | collective-permute-start | bytes 380888 | tf_op jit(solution)/shard_map/while/body/eval_jaxpr/ppermute | solution.py:11
  445.0 12.0 %collective-permute-done.1 = bf16[115,552]{1,0:T(8,128)(2,1)S(1)} collective-permute-done((bf16[115,552]{1,0:T(8,128)(2,1)S(1)}, bf16[115,552]{1,0:T(8,128)(2,1)S(1)}, u32[]{:S(2)}, u32[]{:S(2)}) %collective-permute-start.1) | collective-permute-done | bytes 126992 | tf_op jit(solution)/shard_map/while/body/eval_jaxpr/ppermute | solution.py:11
  457.1 1.9 collective-permute-start
  459.0 20.1 %collective-permute-start.1 = (bf16[115,552]{1,0:T(8,128)(2,1)S(1)}, bf16[115,552]{1,0:T(8,128)(2,1)S(1)}, u32[]{:S(2)}, u32[]{:S(2)}) collective-permute-start(bf16[115,552]{1,0:T(8,128)(2,1)S(1)} %copy.22), channel_id=1, source_target_pairs={{0,60},{4,0},{8,4},{12,8},{16,12},{20,16},{24,20},{28,24},{32,28},... | collective-permute-start | bytes 380888 | tf_op jit(solution)/shard_map/while/body/eval_jaxpr/ppermute | solution.py:11
  479.8 12.2 %collective-permute-done.1 = bf16[115,552]{1,0:T(8,128)(2,1)S(1)} collective-permute-done((bf16[115,552]{1,0:T(8,128)(2,1)S(1)}, bf16[115,552]{1,0:T(8,128)(2,1)S(1)}, u32[]{:S(2)}, u32[]{:S(2)}) %collective-permute-start.1) | collective-permute-done | bytes 126992 | tf_op jit(solution)/shard_map/while/body/eval_jaxpr/ppermute | solution.py:11
  492.7 76.4 %fusion = f32[736,144]{0,1:T(8,128)S(1)} fusion(f32[736,552]{0,1:T(8,128)S(1)} %add.11), kind=kCustom, calls=%all-reduce-scatter | all-reduce-scatter fusion | flops 423937 | bytes 2053120
  569.1 22.7 %collective-permute-start.10 = (bf16[736,18]{0,1:T(8,128)(2,1)S(1)}, bf16[736,18]{0,1:T(8,128)(2,1)S(1)}, u32[]{:S(2)}, u32[]{:S(2)}) collective-permute-start(bf16[736,18]{0,1:T(8,128)(2,1)S(1)} %slice), channel_id=1, source_target_pairs={{0,1},{1,2},{2,3},{4,5},{5,6},{6,7},{8,9},{9,10},{10,11},{12,13},{... | collective-permute-start | bytes 79496
  591.8 1.3 dynamic-slice.4
  594.1 0.7 dynamic-slice_convert_fusion
  (95 shorter events, 13.4 us)
Async XLA Ops:
  0.0 30.0 %copy-start = (bf16[115,736]{1,0:T(8,128)(2,1)S(1)}, bf16[115,736]{1,0:T(8,128)(2,1)}, u32[]{:S(2)}) copy-start(bf16[115,736]{1,0:T(8,128)(2,1)} %param.6) | copy-start | bytes 507844
  2.1 35.0 %collective-permute-start.6 = (bf16[115,552]{0,1:T(8,128)(2,1)S(1)}, bf16[115,552]{0,1:T(8,128)(2,1)S(1)}, u32[]{:S(2)}, u32[]{:S(2)}) collective-permute-start(bf16[115,552]{0,1:T(8,128)(2,1)S(1)} %mul.7), channel_id=1, source_target_pairs={{0,60},{4,0},{8,4},{12,8},{16,12},{20,16},{24,20},{28,24},{32,28},... | collective-permute-start | bytes 380888 | tf_op jit(solution)/shard_map/ppermute | solution.py:11
  30.2 9.9 %collective-permute-start.2 = (bf16[115,736]{0,1:T(8,128)(2,1)S(1)}, bf16[115,736]{0,1:T(8,128)(2,1)S(1)}, u32[]{:S(2)}, u32[]{:S(2)}) collective-permute-start(bf16[115,736]{0,1:T(8,128)(2,1)S(1)} %mul.6), channel_id=1, source_target_pairs={{0,960},{64,0},{128,64},{192,128},{256,192},{320,256},{384,320},{4... | collective-permute-start | bytes 507848 | tf_op jit(solution)/shard_map/ppermute | solution.py:11
  37.1 7.3 %collective-permute-start.7 = (bf16[115,552]{0,1:T(8,128)(2,1)S(1)}, bf16[115,552]{0,1:T(8,128)(2,1)S(1)}, u32[]{:S(2)}, u32[]{:S(2)}) collective-permute-start(bf16[115,552]{0,1:T(8,128)(2,1)S(1)} %broadcast_select_fusion.4), channel_id=1, source_target_pairs={{0,56},{4,60},{8,0},{12,4},{16,8},{20,12},{24,16},{28,20},{32,24},... | collective-permute-start | bytes 380888 | tf_op jit(solution)/shard_map/ppermute | solution.py:11
  40.1 7.8 %collective-permute-start.3 = (bf16[115,736]{0,1:T(8,128)(2,1)S(1)}, bf16[115,736]{0,1:T(8,128)(2,1)S(1)}, u32[]{:S(2)}, u32[]{:S(2)}) collective-permute-start(bf16[115,736]{0,1:T(8,128)(2,1)S(1)} %broadcast_select_fusion), channel_id=1, source_target_pairs={{0,896},{64,960},{128,0},{192,64},{256,128},{320,192},{384,256},{4... | collective-permute-start | bytes 507848 | tf_op jit(solution)/shard_map/ppermute | solution.py:11
  44.5 13.1 %collective-permute-start.8 = (bf16[115,552]{0,1:T(8,128)(2,1)S(1)}, bf16[115,552]{0,1:T(8,128)(2,1)S(1)}, u32[]{:S(2)}, u32[]{:S(2)}) collective-permute-start(bf16[115,552]{0,1:T(8,128)(2,1)S(1)} %broadcast_select_fusion.5), channel_id=1, source_target_pairs={{0,48},{4,52},{8,56},{12,60},{16,0},{20,4},{24,8},{28,12},{32,16},... | collective-permute-start | bytes 380888 | tf_op jit(solution)/shard_map/ppermute | solution.py:11
  48.0 11.5 %collective-permute-start.4 = (bf16[115,736]{0,1:T(8,128)(2,1)S(1)}, bf16[115,736]{0,1:T(8,128)(2,1)S(1)}, u32[]{:S(2)}, u32[]{:S(2)}) collective-permute-start(bf16[115,736]{0,1:T(8,128)(2,1)S(1)} %broadcast_select_fusion.1), channel_id=1, source_target_pairs={{0,768},{64,832},{128,896},{192,960},{256,0},{320,64},{384,128},{4... | collective-permute-start | bytes 507848 | tf_op jit(solution)/shard_map/ppermute | solution.py:11
  57.6 18.3 %collective-permute-start.9 = (bf16[115,552]{0,1:T(8,128)(2,1)S(1)}, bf16[115,552]{0,1:T(8,128)(2,1)S(1)}, u32[]{:S(2)}, u32[]{:S(2)}) collective-permute-start(bf16[115,552]{0,1:T(8,128)(2,1)S(1)} %broadcast_select_fusion.6), channel_id=1, source_target_pairs={{0,32},{4,36},{8,40},{12,44},{16,48},{20,52},{24,56},{28,60},{32,0... | collective-permute-start | bytes 380888 | tf_op jit(solution)/shard_map/ppermute | solution.py:11
  59.6 16.5 %collective-permute-start.5 = (bf16[115,736]{0,1:T(8,128)(2,1)S(1)}, bf16[115,736]{0,1:T(8,128)(2,1)S(1)}, u32[]{:S(2)}, u32[]{:S(2)}) collective-permute-start(bf16[115,736]{0,1:T(8,128)(2,1)S(1)} %broadcast_select_fusion.2), channel_id=1, source_target_pairs={{0,512},{64,576},{128,640},{192,704},{256,768},{320,832},{384,896}... | collective-permute-start | bytes 507848 | tf_op jit(solution)/shard_map/ppermute | solution.py:11
  76.3 41.4 %collective-permute-start = (bf16[115,736]{1,0:T(8,128)(2,1)S(1)}, bf16[115,736]{1,0:T(8,128)(2,1)S(1)}, u32[]{:S(2)}, u32[]{:S(2)}) collective-permute-start(bf16[115,736]{1,0:T(8,128)(2,1)S(1)} %copy.21), channel_id=1, source_target_pairs={{0,960},{64,0},{128,64},{192,128},{256,192},{320,256},{384,320},{4... | collective-permute-start | bytes 507848 | tf_op jit(solution)/shard_map/while/body/eval_jaxpr/ppermute | solution.py:11
  80.6 37.1 %collective-permute-start.1 = (bf16[115,552]{1,0:T(8,128)(2,1)S(1)}, bf16[115,552]{1,0:T(8,128)(2,1)S(1)}, u32[]{:S(2)}, u32[]{:S(2)}) collective-permute-start(bf16[115,552]{1,0:T(8,128)(2,1)S(1)} %copy.22), channel_id=1, source_target_pairs={{0,60},{4,0},{8,4},{12,8},{16,12},{20,16},{24,20},{28,24},{32,28},... | collective-permute-start | bytes 380888 | tf_op jit(solution)/shard_map/while/body/eval_jaxpr/ppermute | solution.py:11
  117.7 29.1 %collective-permute-start = (bf16[115,736]{1,0:T(8,128)(2,1)S(1)}, bf16[115,736]{1,0:T(8,128)(2,1)S(1)}, u32[]{:S(2)}, u32[]{:S(2)}) collective-permute-start(bf16[115,736]{1,0:T(8,128)(2,1)S(1)} %copy.21), channel_id=1, source_target_pairs={{0,960},{64,0},{128,64},{192,128},{256,192},{320,256},{384,320},{4... | collective-permute-start | bytes 507848 | tf_op jit(solution)/shard_map/while/body/eval_jaxpr/ppermute | solution.py:11
  124.7 22.2 %collective-permute-start.1 = (bf16[115,552]{1,0:T(8,128)(2,1)S(1)}, bf16[115,552]{1,0:T(8,128)(2,1)S(1)}, u32[]{:S(2)}, u32[]{:S(2)}) collective-permute-start(bf16[115,552]{1,0:T(8,128)(2,1)S(1)} %copy.22), channel_id=1, source_target_pairs={{0,60},{4,0},{8,4},{12,8},{16,12},{20,16},{24,20},{28,24},{32,28},... | collective-permute-start | bytes 380888 | tf_op jit(solution)/shard_map/while/body/eval_jaxpr/ppermute | solution.py:11
  146.9 24.1 %collective-permute-start = (bf16[115,736]{1,0:T(8,128)(2,1)S(1)}, bf16[115,736]{1,0:T(8,128)(2,1)S(1)}, u32[]{:S(2)}, u32[]{:S(2)}) collective-permute-start(bf16[115,736]{1,0:T(8,128)(2,1)S(1)} %copy.21), channel_id=1, source_target_pairs={{0,960},{64,0},{128,64},{192,128},{256,192},{320,256},{384,320},{4... | collective-permute-start | bytes 507848 | tf_op jit(solution)/shard_map/while/body/eval_jaxpr/ppermute | solution.py:11
  148.8 22.2 %collective-permute-start.1 = (bf16[115,552]{1,0:T(8,128)(2,1)S(1)}, bf16[115,552]{1,0:T(8,128)(2,1)S(1)}, u32[]{:S(2)}, u32[]{:S(2)}) collective-permute-start(bf16[115,552]{1,0:T(8,128)(2,1)S(1)} %copy.22), channel_id=1, source_target_pairs={{0,60},{4,0},{8,4},{12,8},{16,12},{20,16},{24,20},{28,24},{32,28},... | collective-permute-start | bytes 380888 | tf_op jit(solution)/shard_map/while/body/eval_jaxpr/ppermute | solution.py:11
  171.0 24.1 %collective-permute-start = (bf16[115,736]{1,0:T(8,128)(2,1)S(1)}, bf16[115,736]{1,0:T(8,128)(2,1)S(1)}, u32[]{:S(2)}, u32[]{:S(2)}) collective-permute-start(bf16[115,736]{1,0:T(8,128)(2,1)S(1)} %copy.21), channel_id=1, source_target_pairs={{0,960},{64,0},{128,64},{192,128},{256,192},{320,256},{384,320},{4... | collective-permute-start | bytes 507848 | tf_op jit(solution)/shard_map/while/body/eval_jaxpr/ppermute | solution.py:11
  173.0 22.2 %collective-permute-start.1 = (bf16[115,552]{1,0:T(8,128)(2,1)S(1)}, bf16[115,552]{1,0:T(8,128)(2,1)S(1)}, u32[]{:S(2)}, u32[]{:S(2)}) collective-permute-start(bf16[115,552]{1,0:T(8,128)(2,1)S(1)} %copy.22), channel_id=1, source_target_pairs={{0,60},{4,0},{8,4},{12,8},{16,12},{20,16},{24,20},{28,24},{32,28},... | collective-permute-start | bytes 380888 | tf_op jit(solution)/shard_map/while/body/eval_jaxpr/ppermute | solution.py:11
  195.2 24.1 %collective-permute-start = (bf16[115,736]{1,0:T(8,128)(2,1)S(1)}, bf16[115,736]{1,0:T(8,128)(2,1)S(1)}, u32[]{:S(2)}, u32[]{:S(2)}) collective-permute-start(bf16[115,736]{1,0:T(8,128)(2,1)S(1)} %copy.21), channel_id=1, source_target_pairs={{0,960},{64,0},{128,64},{192,128},{256,192},{320,256},{384,320},{4... | collective-permute-start | bytes 507848 | tf_op jit(solution)/shard_map/while/body/eval_jaxpr/ppermute | solution.py:11
  197.1 22.2 %collective-permute-start.1 = (bf16[115,552]{1,0:T(8,128)(2,1)S(1)}, bf16[115,552]{1,0:T(8,128)(2,1)S(1)}, u32[]{:S(2)}, u32[]{:S(2)}) collective-permute-start(bf16[115,552]{1,0:T(8,128)(2,1)S(1)} %copy.22), channel_id=1, source_target_pairs={{0,60},{4,0},{8,4},{12,8},{16,12},{20,16},{24,20},{28,24},{32,28},... | collective-permute-start | bytes 380888 | tf_op jit(solution)/shard_map/while/body/eval_jaxpr/ppermute | solution.py:11
  219.3 28.6 %collective-permute-start = (bf16[115,736]{1,0:T(8,128)(2,1)S(1)}, bf16[115,736]{1,0:T(8,128)(2,1)S(1)}, u32[]{:S(2)}, u32[]{:S(2)}) collective-permute-start(bf16[115,736]{1,0:T(8,128)(2,1)S(1)} %copy.21), channel_id=1, source_target_pairs={{0,960},{64,0},{128,64},{192,128},{256,192},{320,256},{384,320},{4... | collective-permute-start | bytes 507848 | tf_op jit(solution)/shard_map/while/body/eval_jaxpr/ppermute | solution.py:11
  225.7 22.2 %collective-permute-start.1 = (bf16[115,552]{1,0:T(8,128)(2,1)S(1)}, bf16[115,552]{1,0:T(8,128)(2,1)S(1)}, u32[]{:S(2)}, u32[]{:S(2)}) collective-permute-start(bf16[115,552]{1,0:T(8,128)(2,1)S(1)} %copy.22), channel_id=1, source_target_pairs={{0,60},{4,0},{8,4},{12,8},{16,12},{20,16},{24,20},{28,24},{32,28},... | collective-permute-start | bytes 380888 | tf_op jit(solution)/shard_map/while/body/eval_jaxpr/ppermute | solution.py:11
  247.9 24.1 %collective-permute-start = (bf16[115,736]{1,0:T(8,128)(2,1)S(1)}, bf16[115,736]{1,0:T(8,128)(2,1)S(1)}, u32[]{:S(2)}, u32[]{:S(2)}) collective-permute-start(bf16[115,736]{1,0:T(8,128)(2,1)S(1)} %copy.21), channel_id=1, source_target_pairs={{0,960},{64,0},{128,64},{192,128},{256,192},{320,256},{384,320},{4... | collective-permute-start | bytes 507848 | tf_op jit(solution)/shard_map/while/body/eval_jaxpr/ppermute | solution.py:11
  249.8 22.2 %collective-permute-start.1 = (bf16[115,552]{1,0:T(8,128)(2,1)S(1)}, bf16[115,552]{1,0:T(8,128)(2,1)S(1)}, u32[]{:S(2)}, u32[]{:S(2)}) collective-permute-start(bf16[115,552]{1,0:T(8,128)(2,1)S(1)} %copy.22), channel_id=1, source_target_pairs={{0,60},{4,0},{8,4},{12,8},{16,12},{20,16},{24,20},{28,24},{32,28},... | collective-permute-start | bytes 380888 | tf_op jit(solution)/shard_map/while/body/eval_jaxpr/ppermute | solution.py:11
  272.0 24.1 %collective-permute-start = (bf16[115,736]{1,0:T(8,128)(2,1)S(1)}, bf16[115,736]{1,0:T(8,128)(2,1)S(1)}, u32[]{:S(2)}, u32[]{:S(2)}) collective-permute-start(bf16[115,736]{1,0:T(8,128)(2,1)S(1)} %copy.21), channel_id=1, source_target_pairs={{0,960},{64,0},{128,64},{192,128},{256,192},{320,256},{384,320},{4... | collective-permute-start | bytes 507848 | tf_op jit(solution)/shard_map/while/body/eval_jaxpr/ppermute | solution.py:11
  274.0 22.2 %collective-permute-start.1 = (bf16[115,552]{1,0:T(8,128)(2,1)S(1)}, bf16[115,552]{1,0:T(8,128)(2,1)S(1)}, u32[]{:S(2)}, u32[]{:S(2)}) collective-permute-start(bf16[115,552]{1,0:T(8,128)(2,1)S(1)} %copy.22), channel_id=1, source_target_pairs={{0,60},{4,0},{8,4},{12,8},{16,12},{20,16},{24,20},{28,24},{32,28},... | collective-permute-start | bytes 380888 | tf_op jit(solution)/shard_map/while/body/eval_jaxpr/ppermute | solution.py:11
  296.2 24.1 %collective-permute-start = (bf16[115,736]{1,0:T(8,128)(2,1)S(1)}, bf16[115,736]{1,0:T(8,128)(2,1)S(1)}, u32[]{:S(2)}, u32[]{:S(2)}) collective-permute-start(bf16[115,736]{1,0:T(8,128)(2,1)S(1)} %copy.21), channel_id=1, source_target_pairs={{0,960},{64,0},{128,64},{192,128},{256,192},{320,256},{384,320},{4... | collective-permute-start | bytes 507848 | tf_op jit(solution)/shard_map/while/body/eval_jaxpr/ppermute | solution.py:11
  298.1 22.2 %collective-permute-start.1 = (bf16[115,552]{1,0:T(8,128)(2,1)S(1)}, bf16[115,552]{1,0:T(8,128)(2,1)S(1)}, u32[]{:S(2)}, u32[]{:S(2)}) collective-permute-start(bf16[115,552]{1,0:T(8,128)(2,1)S(1)} %copy.22), channel_id=1, source_target_pairs={{0,60},{4,0},{8,4},{12,8},{16,12},{20,16},{24,20},{28,24},{32,28},... | collective-permute-start | bytes 380888 | tf_op jit(solution)/shard_map/while/body/eval_jaxpr/ppermute | solution.py:11
  320.3 27.6 %collective-permute-start = (bf16[115,736]{1,0:T(8,128)(2,1)S(1)}, bf16[115,736]{1,0:T(8,128)(2,1)S(1)}, u32[]{:S(2)}, u32[]{:S(2)}) collective-permute-start(bf16[115,736]{1,0:T(8,128)(2,1)S(1)} %copy.21), channel_id=1, source_target_pairs={{0,960},{64,0},{128,64},{192,128},{256,192},{320,256},{384,320},{4... | collective-permute-start | bytes 507848 | tf_op jit(solution)/shard_map/while/body/eval_jaxpr/ppermute | solution.py:11
  325.7 22.2 %collective-permute-start.1 = (bf16[115,552]{1,0:T(8,128)(2,1)S(1)}, bf16[115,552]{1,0:T(8,128)(2,1)S(1)}, u32[]{:S(2)}, u32[]{:S(2)}) collective-permute-start(bf16[115,552]{1,0:T(8,128)(2,1)S(1)} %copy.22), channel_id=1, source_target_pairs={{0,60},{4,0},{8,4},{12,8},{16,12},{20,16},{24,20},{28,24},{32,28},... | collective-permute-start | bytes 380888 | tf_op jit(solution)/shard_map/while/body/eval_jaxpr/ppermute | solution.py:11
  347.9 24.1 %collective-permute-start = (bf16[115,736]{1,0:T(8,128)(2,1)S(1)}, bf16[115,736]{1,0:T(8,128)(2,1)S(1)}, u32[]{:S(2)}, u32[]{:S(2)}) collective-permute-start(bf16[115,736]{1,0:T(8,128)(2,1)S(1)} %copy.21), channel_id=1, source_target_pairs={{0,960},{64,0},{128,64},{192,128},{256,192},{320,256},{384,320},{4... | collective-permute-start | bytes 507848 | tf_op jit(solution)/shard_map/while/body/eval_jaxpr/ppermute | solution.py:11
  349.8 22.2 %collective-permute-start.1 = (bf16[115,552]{1,0:T(8,128)(2,1)S(1)}, bf16[115,552]{1,0:T(8,128)(2,1)S(1)}, u32[]{:S(2)}, u32[]{:S(2)}) collective-permute-start(bf16[115,552]{1,0:T(8,128)(2,1)S(1)} %copy.22), channel_id=1, source_target_pairs={{0,60},{4,0},{8,4},{12,8},{16,12},{20,16},{24,20},{28,24},{32,28},... | collective-permute-start | bytes 380888 | tf_op jit(solution)/shard_map/while/body/eval_jaxpr/ppermute | solution.py:11
  372.0 24.1 %collective-permute-start = (bf16[115,736]{1,0:T(8,128)(2,1)S(1)}, bf16[115,736]{1,0:T(8,128)(2,1)S(1)}, u32[]{:S(2)}, u32[]{:S(2)}) collective-permute-start(bf16[115,736]{1,0:T(8,128)(2,1)S(1)} %copy.21), channel_id=1, source_target_pairs={{0,960},{64,0},{128,64},{192,128},{256,192},{320,256},{384,320},{4... | collective-permute-start | bytes 507848 | tf_op jit(solution)/shard_map/while/body/eval_jaxpr/ppermute | solution.py:11
  374.0 22.2 %collective-permute-start.1 = (bf16[115,552]{1,0:T(8,128)(2,1)S(1)}, bf16[115,552]{1,0:T(8,128)(2,1)S(1)}, u32[]{:S(2)}, u32[]{:S(2)}) collective-permute-start(bf16[115,552]{1,0:T(8,128)(2,1)S(1)} %copy.22), channel_id=1, source_target_pairs={{0,60},{4,0},{8,4},{12,8},{16,12},{20,16},{24,20},{28,24},{32,28},... | collective-permute-start | bytes 380888 | tf_op jit(solution)/shard_map/while/body/eval_jaxpr/ppermute | solution.py:11
  396.2 25.6 %collective-permute-start = (bf16[115,736]{1,0:T(8,128)(2,1)S(1)}, bf16[115,736]{1,0:T(8,128)(2,1)S(1)}, u32[]{:S(2)}, u32[]{:S(2)}) collective-permute-start(bf16[115,736]{1,0:T(8,128)(2,1)S(1)} %copy.21), channel_id=1, source_target_pairs={{0,960},{64,0},{128,64},{192,128},{256,192},{320,256},{384,320},{4... | collective-permute-start | bytes 507848 | tf_op jit(solution)/shard_map/while/body/eval_jaxpr/ppermute | solution.py:11
  398.1 23.7 %collective-permute-start.1 = (bf16[115,552]{1,0:T(8,128)(2,1)S(1)}, bf16[115,552]{1,0:T(8,128)(2,1)S(1)}, u32[]{:S(2)}, u32[]{:S(2)}) collective-permute-start(bf16[115,552]{1,0:T(8,128)(2,1)S(1)} %copy.22), channel_id=1, source_target_pairs={{0,60},{4,0},{8,4},{12,8},{16,12},{20,16},{24,20},{28,24},{32,28},... | collective-permute-start | bytes 380888 | tf_op jit(solution)/shard_map/while/body/eval_jaxpr/ppermute | solution.py:11
  421.8 35.2 %collective-permute-start = (bf16[115,736]{1,0:T(8,128)(2,1)S(1)}, bf16[115,736]{1,0:T(8,128)(2,1)S(1)}, u32[]{:S(2)}, u32[]{:S(2)}) collective-permute-start(bf16[115,736]{1,0:T(8,128)(2,1)S(1)} %copy.21), channel_id=1, source_target_pairs={{0,960},{64,0},{128,64},{192,128},{256,192},{320,256},{384,320},{4... | collective-permute-start | bytes 507848 | tf_op jit(solution)/shard_map/while/body/eval_jaxpr/ppermute | solution.py:11
  424.2 32.8 %collective-permute-start.1 = (bf16[115,552]{1,0:T(8,128)(2,1)S(1)}, bf16[115,552]{1,0:T(8,128)(2,1)S(1)}, u32[]{:S(2)}, u32[]{:S(2)}) collective-permute-start(bf16[115,552]{1,0:T(8,128)(2,1)S(1)} %copy.22), channel_id=1, source_target_pairs={{0,60},{4,0},{8,4},{12,8},{16,12},{20,16},{24,20},{28,24},{32,28},... | collective-permute-start | bytes 380888 | tf_op jit(solution)/shard_map/while/body/eval_jaxpr/ppermute | solution.py:11
  457.1 34.9 %collective-permute-start = (bf16[115,736]{1,0:T(8,128)(2,1)S(1)}, bf16[115,736]{1,0:T(8,128)(2,1)S(1)}, u32[]{:S(2)}, u32[]{:S(2)}) collective-permute-start(bf16[115,736]{1,0:T(8,128)(2,1)S(1)} %copy.21), channel_id=1, source_target_pairs={{0,960},{64,0},{128,64},{192,128},{256,192},{320,256},{384,320},{4... | collective-permute-start | bytes 507848 | tf_op jit(solution)/shard_map/while/body/eval_jaxpr/ppermute | solution.py:11
  459.0 33.0 %collective-permute-start.1 = (bf16[115,552]{1,0:T(8,128)(2,1)S(1)}, bf16[115,552]{1,0:T(8,128)(2,1)S(1)}, u32[]{:S(2)}, u32[]{:S(2)}) collective-permute-start(bf16[115,552]{1,0:T(8,128)(2,1)S(1)} %copy.22), channel_id=1, source_target_pairs={{0,60},{4,0},{8,4},{12,8},{16,12},{20,16},{24,20},{28,24},{32,28},... | collective-permute-start | bytes 380888 | tf_op jit(solution)/shard_map/while/body/eval_jaxpr/ppermute | solution.py:11
  569.1 24.7 %collective-permute-start.10 = (bf16[736,18]{0,1:T(8,128)(2,1)S(1)}, bf16[736,18]{0,1:T(8,128)(2,1)S(1)}, u32[]{:S(2)}, u32[]{:S(2)}) collective-permute-start(bf16[736,18]{0,1:T(8,128)(2,1)S(1)} %slice), channel_id=1, source_target_pairs={{0,1},{1,2},{2,3},{4,5},{5,6},{6,7},{8,9},{9,10},{10,11},{12,13},{... | collective-permute-start | bytes 79496
where the time goes:
time: 606 us; the launch traced here: 595 us
  starting transfers between devices  432 us (71%)
  blocking collectives  76.4 us (13%)
  waiting for transfers between devices  67.7 us (11%)
  matrix products  10.2 us (2%)
    ppermute x38, starting transfers between devices, passed_along(): lax.ppermute(shard, axis, [(i, (i + by) % count) for i in range(count)])  409 us
    unnamed x1, blocking collectives  76.4 us
    ppermute x38, waiting for transfers between devices, passed_along(): lax.ppermute(shard, axis, [(i, (i + by) % count) for i in range(count)])  67.7 us
    unnamed x1, starting transfers between devices  22.7 us
  transfers between devices with their start and end apart: 39, of which 19 were waited for; matrix products, arithmetic and copies ran while one was open for 2% of the time, Pallas kernels for 0%

commit v1 on v0

v1 whole, which is shorter than its diff:
```python
import functools

import jax
import jax.numpy as jnp
from jax import lax
from jax.experimental import pallas as pl
from jax.experimental.pallas import tpu as pltpu
from jax.sharding import PartitionSpec as P

BLK = 23
KB = 5
PITCH = 24
MB, NB = 32, 24
SLAB_SLOTS, GREEN_SLOTS = 40, 30
SLAB_PER, GREEN_PER = 3, 4
SLAB_TILES, GREEN_TILES = 8, 6
NX, NY, NZ, ZLO = 4, 4, 32, 16
MESH = pl.DeviceIdType.MESH
F32, BF16 = jnp.float32, jnp.bfloat16


def iota(shape, dim):
    return lax.broadcasted_iota(jnp.int32, shape, dim)


def one_hot(where):
    return jnp.where(where, 1.0, 0.0).astype(BF16)


def dot(a, b, dims=((1,), (0,))):
    return lax.dot_general(a, b, (dims, ((), ())), preferred_element_type=F32)


def steps_over(x, edges):
    return sum(jnp.where(x >= e, 1, 0) for e in edges)


def block_codes(mask, blocks, slots, per):
    live = one_hot(mask > 0)
    eye = one_hot(iota((blocks, blocks), 0) == iota((blocks, blocks), 1))
    lower = one_hot(iota((blocks, blocks), 0) >= iota((blocks, blocks), 1))
    live_t = dot(eye, live, ((1,), (1,)))
    live_b = live_t.astype(BF16)
    through = dot(lower, live_b)
    whole = dot(jnp.ones((blocks, blocks), BF16), live_b)
    earlier = dot(whole.astype(BF16), one_hot(iota((KB, KB), 0) < iota((KB, KB), 1)))
    rank = jnp.where(live_t > 0.5, through + earlier - 1.0, -1.0).astype(jnp.int32)
    lane = iota((1, 128), 1)
    slot = lane - slots * steps_over(lane, [slots * q for q in range(1, per)])
    slot = jnp.where(lane < slots * per, slot, -2)
    row = iota((blocks, 128), 0)
    found = jnp.zeros((blocks, 128), F32)
    for kb in range(KB):
        number = (row + (kb * blocks + 1)).astype(F32)
        found = found + jnp.where(rank[:, kb : kb + 1] == slot, number, 0.0)
    return jnp.sum(found, axis=0, keepdims=True).astype(jnp.int32) - 1


def pack(piece, mask, blocks, slots, per, tiles, rows_ref):
    code = block_codes(mask, blocks, slots, per)
    kb = steps_over(code, [blocks * q for q in range(1, KB)])
    block = code - blocks * kb
    lane = iota((1, 128), 1)
    inner = steps_over(lane, [slots * q for q in range(1, per)])
    width = blocks * BLK
    row = iota((width, 128), 0)
    last = iota((PITCH, 128), 0) == BLK
    out = []
    for tile in range(tiles):
        i = per * tile + inner
        source = jnp.where((code >= 0) & (i < BLK), block * BLK + i, -1)
        rows_ref[pl.ds(0, KB * BLK), :] = dot(piece, one_hot(row == source))
        packed = jnp.zeros((PITCH, 128), F32)
        for q in range(KB):
            part = rows_ref[pl.ds(BLK * q, PITCH), :]
            packed = packed + jnp.where(kb == q, part, 0.0)
        out.append(jnp.where(last, code.astype(F32), packed))
    return jnp.concatenate(out, axis=1)


def spread_rows(packet, kb):
    data = iota((PITCH, 256), 0) < BLK
    parts = [jnp.where(data & (kb == q), packet, 0.0) for q in range(KB)]
    parts.append(jnp.zeros((128 - KB * PITCH, 256), F32))
    return jnp.concatenate(parts, axis=0).astype(BF16)


def decode(row, blocks, slots, per):
    code = row.astype(jnp.int32)
    kb = steps_over(code, [blocks * q for q in range(1, KB)])
    lane = iota((1, 256), 1)
    tile = jnp.where(lane >= 128, 1, 0)
    inner = per * tile + steps_over(lane - 128 * tile, [slots * q for q in range(1, per)])
    return code, kb, code - blocks * kb, inner


def unpack_slab(packet):
    code, kb, mb, inner = decode(packet[BLK : BLK + 1, :256], MB, SLAB_SLOTS, SLAB_PER)
    at = jnp.where(code >= 0, inner * MB + mb, -1000)
    row = iota((256, 256), 0)
    low, high = one_hot(row == at), one_hot(row == at + 64)
    groups = [spread_rows(packet[:, 256 * g : 256 * g + 256], kb) for g in range(4)]
    even = dot(jnp.concatenate([groups[0], groups[2]], axis=0), low, ((1,), (1,)))
    odd = dot(jnp.concatenate([groups[1], groups[3]], axis=0), high, ((1,), (1,)))
    out = []
    for h in range(2):
        e, o = even[128 * h : 128 * h + 128], odd[128 * h : 128 * h + 128]
        out += [e[:, :128], e[:, 128:] + o[:, :128], o[:, 128:]]
    return jnp.concatenate(out, axis=1).astype(BF16)


def unpack_green(packet, half):
    code, kb, nb, inner = decode(packet[BLK : BLK + 1, :256], NB, GREEN_SLOTS, GREEN_PER)
    nb = nb - 12 * half
    core = jnp.where(nb >= 6, 1, 0)
    ours = (code >= 0) & (nb >= 0) & (nb < 12)
    at = jnp.where(ours, core * 64 + inner * 6 + nb - 6 * core, -1000)
    place = one_hot(iota((128, 256), 0) == at)
    rows = [spread_rows(packet[:, 256 * g : 256 * g + 256], kb) for g in range(3)]
    out = dot(jnp.concatenate(rows, axis=0), place, ((1,), (1,)))
    return jnp.concatenate([out[128 * g : 128 * g + 128] for g in range(3)], axis=1).astype(BF16)


def put_back(total):
    lane = iota((1, 768), 1)
    source = jnp.where(lane < MB * BLK, (lane % MB) * BLK + lane // MB, -1)
    rows = dot(one_hot(iota((MB * BLK, 768), 0) == source), total, ((1,), (1,)))
    column = iota((1, 6 * BLK), 1)
    nb = steps_over(column, [BLK * q for q in range(1, 6)])
    j = column - BLK * nb
    source = (j // 8) * 64 + (j % 8) * 6 + nb
    return dot(rows.astype(BF16), one_hot(iota((192, 6 * BLK), 0) == source)).astype(BF16)


def kernel(
    slab, green, mask_slab, mask_green, out,
    sbuf, gbuf, relay, slab_all, green_all, acc, other, rows_ref,
    ring_send, ring_recv, hop_send, relay_recv, far_recv, xy_send, xy_recv, pair_sems,
):
    grid_row, zlo, layer = (lax.axis_index(a) for a in ("row", "col", "layer"))
    x, y = grid_row // NY, grid_row % NY
    hi, core = layer // 2, layer % 2
    z = hi * ZLO + zlo
    away = 1 - hi

    def device(xx, yy, zz, cc):
        return (xx * NY + yy, zz % ZLO, (zz // ZLO) * 2 + cc)

    def along(d):
        return device(x, y, (z + d + NZ) % NZ, core)

    beside_x = [device((x + d) % NX, y, z, core) for d in (1, 3, 2)]
    beside_y = [device(x, (y + d) % NY, z, core) for d in (1, 3, 2)]
    sibling = device(x, y, z, 1 - core)
    hops = (8, -8)

    barrier = pltpu.get_barrier_semaphore()
    partners = [along(1), along(-1), along(8), along(-8), *beside_x, *beside_y, sibling]
    for partner in partners:
        pl.semaphore_signal(barrier, inc=1, device_id=partner, device_id_type=MESH)

    def copy(src, dst, send, recv, to):
        return pltpu.make_async_remote_copy(
            src_ref=src, dst_ref=dst, send_sem=send, recv_sem=recv, device_id=to, device_id_type=MESH
        )

    turn = 1 - 2 * core

    def origin(way, step):
        return (z + (2 * way - 1) * turn * step + 2 * NZ) % NZ

    def ring(way, step):
        slot = origin(way, step)
        return copy(
            gbuf.at[slot], gbuf.at[slot], ring_send.at[way, step], ring_recv.at[slot],
            along((1 - 2 * way) * turn),
        )

    def first_hop(side):
        return copy(
            sbuf.at[hi, grid_row, side], relay.at[side], hop_send.at[0, side], relay_recv.at[side], along(hops[side])
        )

    def second_hop(side):
        origin_hi = ((z - hops[side] + NZ) % NZ) // ZLO
        return copy(
            relay.at[side], sbuf.at[origin_hi, grid_row, side], hop_send.at[1, side], far_recv.at[side], along(hops[side])
        )

    def over_x(which, d):
        slot = sbuf.at[which, grid_row]
        return copy(slot, slot, xy_send.at[which, 0, d], xy_recv.at[which, grid_row], beside_x[d])

    def over_y(which, xx, d):
        row = xx * NY + y
        slot = sbuf.at[which, row]
        return copy(slot, slot, xy_send.at[which, 1 + xx, d], xy_recv.at[which, row], beside_y[d])

    def arrived(which, row):
        slot = sbuf.at[which, row]
        copy(slot, slot, xy_send.at[0, 0, 0], xy_recv.at[which, row], sibling).wait_recv()

    def spread_x(which):
        for d in range(3):
            over_x(which, d).start()

    def spread_y(which):
        for d in (1, 2, 3):
            arrived(which, ((x + d) % NX) * NY + y)
        for d in range(3):
            for xx in range(NX):
                over_y(which, xx, d).start()

    def wait_y(which):
        for d in (1, 2, 3):
            for xx in range(NX):
                arrived(which, xx * NY + (y + d) % NY)

    def take_slab(which, row):
        upper = sbuf[which, row, 0].astype(F32)
        lower = sbuf[which, row, 1].astype(F32)
        packet = jnp.concatenate([upper[:PITCH], upper[PITCH:], lower[:PITCH], lower[PITCH:]], axis=1)
        at = pl.multiple_of((which * 16 + row) * 128, 128)
        slab_all[pl.ds(at, 128), :] = unpack_slab(packet)

    def take_green(slot):
        both = gbuf[slot].astype(F32)
        packet = jnp.concatenate([both[:PITCH], both[PITCH:]], axis=1)
        at = pl.multiple_of(slot * 128, 128)
        green_all[pl.ds(at, 128), :] = unpack_green(packet, hi)

    rows_ref[...] = jnp.zeros_like(rows_ref)
    packet = pack(green[...], mask_green[...], NB, GREEN_SLOTS, GREEN_PER, GREEN_TILES, rows_ref)
    gbuf[z] = jnp.concatenate([packet[:, :384], packet[:, 384:]], axis=0).astype(BF16)
    pl.semaphore_wait(barrier, len(partners))
    ring(0, 0).start()
    ring(1, 0).start()

    packet = pack(slab[...], mask_slab[...], MB, SLAB_SLOTS, SLAB_PER, SLAB_TILES, rows_ref)
    for side in range(2):
        quarters = [packet[:, 512 * side + 256 * g : 512 * side + 256 * g + 256] for g in range(2)]
        sbuf[hi, grid_row, side] = jnp.concatenate(quarters, axis=0).astype(BF16)
    first_hop(0).start()
    first_hop(1).start()
    spread_x(hi)
    take_green(z)

    def advance(step, carry):
        copy(gbuf.at[0], gbuf.at[0], ring_send.at[0, 0], ring_recv.at[origin(0, step)], sibling).wait_recv()
        ring(0, step).start()
        copy(gbuf.at[0], gbuf.at[0], ring_send.at[0, 0], ring_recv.at[origin(1, step)], sibling).wait_recv()

        @pl.when(step < 15)
        def _():
            ring(1, step).start()

        @pl.when(step == 2)
        def _():
            spread_y(hi)

        @pl.when(step == 4)
        def _():
            for side in range(2):
                first_hop(side).wait_recv()
                second_hop(side).start()

        @pl.when(step == 5)
        def _():
            wait_y(hi)

        @pl.when(step == 8)
        def _():
            for side in range(2):
                second_hop(side).wait_recv()
            spread_x(away)

        @pl.when(step == 10)
        def _():
            spread_y(away)

        @pl.when(step == 13)
        def _():
            wait_y(away)

        take_green(origin(0, step))
        take_green(origin(1, step))

        @pl.when((step >= 5) & (step < 13))
        def _():
            take_slab(hi, 2 * (step - 5))
            take_slab(hi, 2 * (step - 5) + 1)

        return carry

    lax.fori_loop(1, 16, advance, 0)
    copy(gbuf.at[0], gbuf.at[0], ring_send.at[0, 0], ring_recv.at[origin(0, 16)], sibling).wait_recv()
    take_green(origin(0, 16))

    def rest(row, carry):
        take_slab(away, row)
        return carry

    lax.fori_loop(0, 16, rest, 0)

    acc[...] = jnp.zeros_like(acc)

    def multiply(part, carry):
        at = pl.multiple_of(part * 512, 512)
        left = slab_all[pl.ds(at, 512), :]
        for g in range(3):
            term = dot(green_all[pl.ds(at, 512), 128 * g : 128 * g + 128], left, ((0,), (0,)))
            acc[0, 64 * g : 64 * g + 64, :] += term[:64]
            acc[1, 64 * g : 64 * g + 64, :] += term[64:]
        return carry

    lax.fori_loop(0, 8, multiply, 0)
    swap = copy(acc.at[1 - core], other, pair_sems.at[0], pair_sems.at[1], sibling)
    swap.start()
    swap.wait()
    out[...] = put_back((acc[core] + other[...]).astype(BF16))

    def sent(step, carry):
        ring(0, step).wait_send()

        @pl.when(step < 15)
        def _():
            ring(1, step).wait_send()

        return carry

    lax.fori_loop(0, 16, sent, 0)
    for side in range(2):
        first_hop(side).wait_send()
        second_hop(side).wait_send()
    for which in range(2):
        for d in range(3):
            over_x(which, d).wait_send()
            for xx in range(NX):
                over_y(which, xx, d).wait_send()


def shards(slab, green, mask_slab, mask_green):
    vmem = pl.BlockSpec(memory_space=pltpu.VMEM)
    dma = pltpu.SemaphoreType.DMA
    return pl.pallas_call(
        kernel,
        out_shape=jax.ShapeDtypeStruct((MB * BLK, 6 * BLK), BF16),
        in_specs=[vmem] * 4,
        out_specs=vmem,
        scratch_shapes=[
            pltpu.VMEM((2, 16, 2, 2 * PITCH, 256), BF16),
            pltpu.VMEM((NZ, 2 * PITCH, 384), BF16),
            pltpu.VMEM((2, 2 * PITCH, 256), BF16),
            pltpu.VMEM((32 * 128, 768), BF16),
            pltpu.VMEM((32 * 128, 384), BF16),
            pltpu.VMEM((2, 192, 768), F32),
            pltpu.VMEM((192, 768), F32),
            pltpu.VMEM((120, 128), F32),
            dma((2, 16)),
            dma((NZ,)),
            dma((2, 2)),
            dma((2,)),
            dma((2,)),
            dma((2, 5, 3)),
            dma((2, 16)),
            dma((2,)),
        ],
        compiler_params=pltpu.CompilerParams(
            collective_id=0, has_side_effects=True, vmem_limit_bytes=48 * 1024 * 1024
        ),
        name="block_sparse_product",
    )(slab, green, mask_slab, mask_green)


def solution(mesh):
    in_specs = (
        P(("layer", "row"), "col"),
        P(("layer", "col"), "row"),
        P(("layer", "row"), "col"),
        P(("layer", "col"), "row"),
    )
    out_specs = P("col", ("row", "layer"))
    return jax.shard_map(shards, mesh=mesh, in_specs=in_specs, out_specs=out_specs, check_vma=False)
```

time: 606 us -> 92.5 us (0.15); the launches traced: 595 us -> 92.4 us
  starting transfers between devices: 432 us -> 0 us
  Pallas kernels: 0 us -> 90.4 us
  blocking collectives: 76.4 us -> 0 us
  waiting for transfers between devices: 67.7 us -> 0 us
  matrix products: 10.2 us -> 0 us
    ppermute x38 -> x0, starting transfers between devices: 409 us -> none  [passed_along(): lax.ppermute(shard, axis, [(i, (i + by) % count) for i in range(count)])]
    pallas_call x0 -> x1, Pallas kernels: none -> 90.4 us  [shards(): pl.pallas_call(kernel, out_shape=jax.ShapeDtypeStruct((MB * BLK, 6 * BLK)...]
    unnamed x1 -> x0, blocking collectives: 76.4 us -> none
    ppermute x38 -> x0, waiting for transfers between devices: 67.7 us -> none  [passed_along(): lax.ppermute(shard, axis, [(i, (i + by) % count) for i in range(count)])]
    unnamed x1 -> x0, starting transfers between devices: 22.7 us -> none
    dot_general x16 -> x0, matrix products: 10.2 us -> none  [contract(): lax.dot_general(left, right, (((0,), (0,)), ((), ())), preferred_element_...]
  transfers between devices with their start and end apart: 39 -> 0, of which waited for: 19 -> 0; matrix products, arithmetic and copies ran while one was open for 2% -> 0% of each run, Pallas kernels for 0% -> 0%
where the time goes in v1:
time: 92.5 us; the launch traced here: 92.4 us
  Pallas kernels  90.4 us (98%)
  local copies, waits for them, and re-layouts  1.95 us (2%)
    pallas_call x1, Pallas kernels, shards(): pl.pallas_call(kernel, out_shape=jax.ShapeDtypeStruct((MB * BLK, 6 * BLK)...  90.4 us

profile of v1, /device:TPU:1, one launch (start us, length us, event | category | flops | bytes accessed | tf_op | source)
XLA Modules:
  0.0 92.4 jit_solution(11265323812756301557)
XLA Ops:
  0.0 0.0 copy-start.2
  0.0 0.0 copy-start.1
  0.0 0.0 copy-start
  0.0 1.1 %copy.5.green = bf16[115,552]{1,0:T(8,128)(2,1)S(1)} copy(bf16[115,552]{0,1:T(8,128)(2,1)} %param.5) | data formatting | bytes 253920 | tf_op args[1]
  1.1 0.0 copy-done.2
  1.1 0.0 copy-done.1
  1.1 0.0 copy-done
  1.1 90.4 %block_sparse_product.1 = bf16[736,138]{1,0:T(8,128)(2,1)S(1)} custom-call(bf16[115,736]{1,0:T(8,128)(2,1)S(1)} %copy-done, bf16[115,552]{1,0:T(8,128)(2,1)S(1)} %copy.5.green, s32[5,32]{1,0:T(8,128)S(1)} %copy-done.1, s32[5,24]{1,0:T(8,128)S(1)} %copy-done.2), custom_call_target="tpu_custom_call" | custom-call | tf_op jit(solution)/shard_map/block_sparse_product/pallas_call | solution.py:345
  91.6 0.8 copy.6
Async XLA Ops:
  0.0 1.1 %copy-start.2 = (s32[5,24]{1,0:T(8,128)S(1)}, s32[5,24]{1,0:T(8,128)}, u32[]{:S(2)}) copy-start(s32[5,24]{1,0:T(8,128)} %mask_green.1) | copy-start | bytes 1444
  0.0 1.1 %copy-start.1 = (s32[5,32]{1,0:T(8,128)S(1)}, s32[5,32]{1,0:T(8,128)}, u32[]{:S(2)}) copy-start(s32[5,32]{1,0:T(8,128)} %mask_slab.1) | copy-start | bytes 1924
  0.0 1.1 %copy-start = (bf16[115,736]{1,0:T(8,128)(2,1)S(1)}, bf16[115,736]{1,0:T(8,128)(2,1)}, u32[]{:S(2)}) copy-start(bf16[115,736]{1,0:T(8,128)(2,1)} %slab.1) | copy-start | bytes 507844

commit v2 on v1

v2 whole, which is shorter than its diff:
```python
import functools

import jax
import jax.numpy as jnp
from jax import lax
from jax.experimental import pallas as pl
from jax.experimental.pallas import tpu as pltpu
from jax.sharding import PartitionSpec as P

BLK = 23
KB = 5
PITCH = 24
MB, NB = 32, 24
SLAB_SLOTS, GREEN_SLOTS = 40, 30
SLAB_PER, GREEN_PER = 3, 4
SLAB_TILES, GREEN_TILES = 8, 6
NX, NY, NZ, ZLO = 4, 4, 32, 16
MESH = pl.DeviceIdType.MESH
F32, BF16 = jnp.float32, jnp.bfloat16


def iota(shape, dim):
    return lax.broadcasted_iota(jnp.int32, shape, dim)


def one_hot(where):
    return jnp.where(where, 1.0, 0.0).astype(BF16)


def dot(a, b, dims=((1,), (0,))):
    return lax.dot_general(a, b, (dims, ((), ())), preferred_element_type=F32)


def steps_over(x, edges):
    return sum(jnp.where(x >= e, 1, 0) for e in edges)


def block_codes(mask, blocks, slots, per):
    live = one_hot(mask > 0)
    eye = one_hot(iota((blocks, blocks), 0) == iota((blocks, blocks), 1))
    lower = one_hot(iota((blocks, blocks), 0) >= iota((blocks, blocks), 1))
    live_t = dot(eye, live, ((1,), (1,)))
    live_b = live_t.astype(BF16)
    through = dot(lower, live_b)
    whole = dot(jnp.ones((blocks, blocks), BF16), live_b)
    earlier = dot(whole.astype(BF16), one_hot(iota((KB, KB), 0) < iota((KB, KB), 1)))
    rank = jnp.where(live_t > 0.5, through + earlier - 1.0, -1.0).astype(jnp.int32)
    lane = iota((1, 128), 1)
    slot = lane - slots * steps_over(lane, [slots * q for q in range(1, per)])
    slot = jnp.where(lane < slots * per, slot, -2)
    row = iota((blocks, 128), 0)
    found = jnp.zeros((blocks, 128), F32)
    for kb in range(KB):
        number = (row + (kb * blocks + 1)).astype(F32)
        found = found + jnp.where(rank[:, kb : kb + 1] == slot, number, 0.0)
    return jnp.sum(found, axis=0, keepdims=True).astype(jnp.int32) - 1


def pack(piece, mask, blocks, slots, per, tiles, rows_ref, along):
    code = block_codes(mask, blocks, slots, per)
    kb = steps_over(code, [blocks * q for q in range(1, KB)])
    block = code - blocks * kb
    lane = iota((1, 128), 1)
    inner = steps_over(lane, [slots * q for q in range(1, per)])
    width = blocks * BLK
    row = iota((width, 128), 0)
    last = iota((PITCH, 128), 0) == BLK
    out = []
    for tile in range(tiles):
        i = per * tile + inner
        source = jnp.where((code >= 0) & (i < BLK), block * BLK + i, -1)
        rows_ref[pl.ds(0, KB * BLK), :] = dot(piece, one_hot(row == source), ((along,), (0,)))
        packed = jnp.zeros((PITCH, 128), F32)
        for q in range(KB):
            part = rows_ref[pl.ds(BLK * q, PITCH), :]
            packed = packed + jnp.where(kb == q, part, 0.0)
        out.append(jnp.where(last, code.astype(F32), packed))
    return jnp.concatenate(out, axis=1)


def spread_rows(packet, kb):
    data = iota((PITCH, 256), 0) < BLK
    parts = [jnp.where(data & (kb == q), packet, 0.0) for q in range(KB)]
    parts.append(jnp.zeros((128 - KB * PITCH, 256), F32))
    return jnp.concatenate(parts, axis=0).astype(BF16)


def decode(row, blocks, slots, per):
    code = row.astype(jnp.int32)
    kb = steps_over(code, [blocks * q for q in range(1, KB)])
    lane = iota((1, 256), 1)
    tile = jnp.where(lane >= 128, 1, 0)
    inner = per * tile + steps_over(lane - 128 * tile, [slots * q for q in range(1, per)])
    return code, kb, code - blocks * kb, inner


def unpack_slab(packet):
    code, kb, mb, inner = decode(packet[BLK : BLK + 1, :256], MB, SLAB_SLOTS, SLAB_PER)
    at = jnp.where(code >= 0, inner * MB + mb, -1000)
    row = iota((256, 256), 0)
    low, high = one_hot(row == at), one_hot(row == at + 64)
    groups = [spread_rows(packet[:, 256 * g : 256 * g + 256], kb) for g in range(4)]
    even = dot(jnp.concatenate([groups[0], groups[2]], axis=0), low, ((1,), (1,)))
    odd = dot(jnp.concatenate([groups[1], groups[3]], axis=0), high, ((1,), (1,)))
    out = []
    for h in range(2):
        e, o = even[128 * h : 128 * h + 128], odd[128 * h : 128 * h + 128]
        out += [e[:, :128], e[:, 128:] + o[:, :128], o[:, 128:]]
    return jnp.concatenate(out, axis=1).astype(BF16)


def unpack_green(packet, half):
    code, kb, nb, inner = decode(packet[BLK : BLK + 1, :256], NB, GREEN_SLOTS, GREEN_PER)
    nb = nb - 12 * half
    core = jnp.where(nb >= 6, 1, 0)
    ours = (code >= 0) & (nb >= 0) & (nb < 12)
    at = jnp.where(ours, core * 64 + inner * 6 + nb - 6 * core, -1000)
    place = one_hot(iota((128, 256), 0) == at)
    rows = [spread_rows(packet[:, 256 * g : 256 * g + 256], kb) for g in range(3)]
    out = dot(jnp.concatenate(rows, axis=0), place, ((1,), (1,)))
    return jnp.concatenate([out[128 * g : 128 * g + 128] for g in range(3)], axis=1).astype(BF16)


def columns_back():
    lane = iota((1, MB * BLK), 1)
    mb = (lane * 2850) // 65536
    return one_hot(iota((768, MB * BLK), 0) == (lane - BLK * mb) * MB + mb)


def put_back(total, order):
    row = iota((6 * BLK, 192), 0)
    nb = steps_over(row, [BLK * q for q in range(1, 6)])
    j = row - BLK * nb
    source = (j // 8) * 64 + (j % 8) * 6 + nb
    rows = dot(one_hot(iota((6 * BLK, 192), 1) == source), total)
    return dot(rows.astype(BF16), order).astype(BF16)


def kernel(
    slab, green, mask_slab, mask_green, out,
    sbuf, gbuf, relay, slab_all, green_all, acc, other, rows_ref, order,
    chain_send, near_send, ring_recv, hop_send, relay_recv, far_recv, xy_send, xy_recv, pair_sems,
):
    grid_row, zlo, layer = (lax.axis_index(a) for a in ("row", "col", "layer"))
    x, y = grid_row // NY, grid_row % NY
    hi, core = layer // 2, layer % 2
    z = hi * ZLO + zlo
    away = 1 - hi

    def device(xx, yy, zz, cc):
        return (xx * NY + yy, zz % ZLO, (zz // ZLO) * 2 + cc)

    def along(d):
        return device(x, y, (z + d + NZ) % NZ, core)

    beside_x = [device((x + d) % NX, y, z, core) for d in (1, 3, 2)]
    beside_y = [device(x, (y + d) % NY, z, core) for d in (1, 3, 2)]
    sibling = device(x, y, z, 1 - core)
    hops = (8, -8)

    barrier = pltpu.get_barrier_semaphore()
    partners = [*(along(d) for d in (1, -1, 3, -3, 8, -8)), *beside_x, *beside_y, sibling]
    for partner in partners:
        pl.semaphore_signal(barrier, inc=1, device_id=partner, device_id_type=MESH)

    def copy(src, dst, send, recv, to):
        return pltpu.make_async_remote_copy(
            src_ref=src, dst_ref=dst, send_sem=send, recv_sem=recv, device_id=to, device_id_type=MESH
        )

    turn = 1 - 2 * core

    def slot_at(off):
        return (z + turn * off + 2 * NZ) % NZ

    def send_green(off, d, sem):
        slot = slot_at(off)
        return copy(gbuf.at[slot], gbuf.at[slot], sem, ring_recv.at[slot], along(turn * d))

    def chain(way, step):
        sign = 2 * way - 1
        return send_green(sign * 3 * step, -3 * sign, chain_send.at[way, step])

    def near(way, step, d):
        return send_green((2 * way - 1) * 3 * step, d, near_send.at[way, step, (d + 1) // 2])

    def green_arrived(off):
        copy(gbuf.at[0], gbuf.at[0], chain_send.at[0, 0], ring_recv.at[slot_at(off)], sibling).wait_recv()

    def first_hop(side):
        return copy(
            sbuf.at[hi, grid_row, side], relay.at[side], hop_send.at[0, side], relay_recv.at[side], along(hops[side])
        )

    def second_hop(side):
        origin_hi = ((z - hops[side] + NZ) % NZ) // ZLO
        return copy(
            relay.at[side], sbuf.at[origin_hi, grid_row, side], hop_send.at[1, side], far_recv.at[side], along(hops[side])
        )

    def send_slab(which, row, half, sem, to):
        part = sbuf.at[which, row, half]
        return copy(part, part, sem, xy_recv.at[which, row, half], to)

    def first_phase(which, d):
        return [
            send_slab(which, grid_row, 0, xy_send.at[which, 0, 0, d], beside_x[d]),
            send_slab(which, grid_row, 1, xy_send.at[which, 1, 0, d], beside_y[d]),
        ]

    def second_phase(which, q, d):
        return [
            send_slab(which, ((x + q) % NX) * NY + y, 0, xy_send.at[which, 0, 1 + q, d], beside_y[d]),
            send_slab(which, x * NY + (y + q) % NY, 1, xy_send.at[which, 1, 1 + q, d], beside_x[d]),
        ]

    def slab_arrived(which, row, half):
        part = sbuf.at[which, row, half]
        copy(part, part, xy_send.at[0, 0, 0, 0], xy_recv.at[which, row, half], sibling).wait_recv()

    def start_first(which):
        for d in range(3):
            for c in first_phase(which, d):
                c.start()

    def start_second(which):
        for d in (1, 2, 3):
            slab_arrived(which, ((x + d) % NX) * NY + y, 0)
            slab_arrived(which, x * NY + (y + d) % NY, 1)
        for d in range(3):
            for q in range(4):
                for c in second_phase(which, q, d):
                    c.start()

    def wait_second(which):
        for q in range(4):
            for d in (1, 2, 3):
                slab_arrived(which, ((x + q) % NX) * NY + (y + d) % NY, 0)
                slab_arrived(which, ((x + d) % NX) * NY + (y + q) % NY, 1)

    def take_slab(which, row):
        upper = sbuf[which, row, 0].astype(F32)
        lower = sbuf[which, row, 1].astype(F32)
        packet = jnp.concatenate([upper[:PITCH], upper[PITCH:], lower[:PITCH], lower[PITCH:]], axis=1)
        at = pl.multiple_of((which * 16 + row) * 128, 128)
        slab_all[pl.ds(at, 128), :] = unpack_slab(packet)

    def take_green(off):
        slot = slot_at(off)
        both = gbuf[slot].astype(F32)
        packet = jnp.concatenate([both[:PITCH], both[PITCH:]], axis=1)
        at = pl.multiple_of(slot * 128, 128)
        green_all[pl.ds(at, 128), :] = unpack_green(packet, hi)

    def multiply(part):
        at = pl.multiple_of(part * 512, 512)
        left = slab_all[pl.ds(at, 512), :]
        for g in range(3):
            term = dot(green_all[pl.ds(at, 512), 128 * g : 128 * g + 128], left, ((0,), (0,)))
            acc[0, 64 * g : 64 * g + 64, :] += term[:64]
            acc[1, 64 * g : 64 * g + 64, :] += term[64:]

    def loop(start, stop, body):
        lax.fori_loop(start, stop, lambda i, carry: (body(i), carry)[1], 0)

    rows_ref[...] = jnp.zeros_like(rows_ref)
    packet = pack(green[...], mask_green[...], NB, GREEN_SLOTS, GREEN_PER, GREEN_TILES, rows_ref, 0)
    gbuf[z] = jnp.concatenate([packet[:, :384], packet[:, 384:]], axis=0).astype(BF16)
    packet = pack(slab[...], mask_slab[...], MB, SLAB_SLOTS, SLAB_PER, SLAB_TILES, rows_ref, 1)
    for side in range(2):
        quarters = [packet[:, 512 * side + 256 * g : 512 * side + 256 * g + 256] for g in range(2)]
        sbuf[hi, grid_row, side] = jnp.concatenate(quarters, axis=0).astype(BF16)
    pl.semaphore_wait(barrier, len(partners))
    chain(0, 0).start()
    chain(1, 0).start()
    first_hop(0).start()
    first_hop(1).start()
    near(0, 0, 1).start()
    near(0, 0, -1).start()
    start_first(hi)
    order[...] = columns_back()
    acc[...] = jnp.zeros_like(acc)
    take_green(0)

    def advance(step):
        green_arrived(-3 * step)

        @pl.when(step < 5)
        def _():
            chain(0, step).start()

        near(0, step, 1).start()
        near(0, step, -1).start()
        green_arrived(3 * step)

        @pl.when(step < 5)
        def _():
            chain(1, step).start()
            near(1, step, -1).start()

        near(1, step, 1).start()

        @pl.when(step == 1)
        def _():
            start_second(hi)

        @pl.when(step == 2)
        def _():
            for side in range(2):
                first_hop(side).wait_recv()
                second_hop(side).start()

        @pl.when(step == 3)
        def _():
            for side in range(2):
                second_hop(side).wait_recv()
            start_first(away)
            wait_second(hi)

        @pl.when(step == 4)
        def _():
            start_second(away)

        take_green(-3 * step)
        take_green(3 * step)
        before = 3 * (step - 1)
        green_arrived(-before - 1)
        take_green(-before - 1)
        green_arrived(before + 1)
        take_green(before + 1)

        @pl.when(step > 1)
        def _():
            green_arrived(1 - before)
            take_green(1 - before)
            green_arrived(before - 1)
            take_green(before - 1)

        @pl.when(step == 3)
        def _():
            loop(0, 6, lambda row: take_slab(hi, row))

        @pl.when(step == 4)
        def _():
            loop(6, 11, lambda row: take_slab(hi, row))

        @pl.when(step == 5)
        def _():
            loop(11, 16, lambda row: take_slab(hi, row))

    loop(1, 6, advance)
    for off in (-16, -14, 14):
        green_arrived(off)
        take_green(off)
    loop(0, 4, lambda part: multiply(4 * hi + part))
    wait_second(away)
    loop(0, 16, lambda row: take_slab(away, row))
    loop(0, 4, lambda part: multiply(4 * away + part))

    swap = copy(acc.at[1 - core], other, pair_sems.at[0], pair_sems.at[1], sibling)
    swap.start()
    swap.wait()
    out[...] = put_back((acc[core] + other[...]).astype(BF16), order[...])

    for way in range(2):
        for step in range(5):
            chain(way, step).wait_send()
        for step in range(6):
            for d in (-1, 1):
                if (step > 0 or way == 0) and not (way == 1 and step == 5 and d == -1):
                    near(way, step, d).wait_send()
    for side in range(2):
        first_hop(side).wait_send()
        second_hop(side).wait_send()
    for which in range(2):
        for d in range(3):
            for c in first_phase(which, d):
                c.wait_send()
            for q in range(4):
                for c in second_phase(which, q, d):
                    c.wait_send()


def shards(slab, green, mask_slab, mask_green):
    vmem = pl.BlockSpec(memory_space=pltpu.VMEM)
    dma = pltpu.SemaphoreType.DMA
    product = pl.pallas_call(
        kernel,
        out_shape=jax.ShapeDtypeStruct((6 * BLK, MB * BLK), BF16),
        in_specs=[vmem] * 4,
        out_specs=vmem,
        scratch_shapes=[
            pltpu.VMEM((2, 16, 2, 2 * PITCH, 256), BF16),
            pltpu.VMEM((NZ, 2 * PITCH, 384), BF16),
            pltpu.VMEM((2, 2 * PITCH, 256), BF16),
            pltpu.VMEM((32 * 128, 768), BF16),
            pltpu.VMEM((32 * 128, 384), BF16),
            pltpu.VMEM((2, 192, 768), F32),
            pltpu.VMEM((192, 768), F32),
            pltpu.VMEM((120, 128), F32),
            pltpu.VMEM((768, MB * BLK), BF16),
            dma((2, 5)),
            dma((2, 6, 2)),
            dma((NZ,)),
            dma((2, 2)),
            dma((2,)),
            dma((2,)),
            dma((2, 2, 5, 3)),
            dma((2, 16, 2)),
            dma((2,)),
        ],
        compiler_params=pltpu.CompilerParams(
            collective_id=0, has_side_effects=True, vmem_limit_bytes=48 * 1024 * 1024
        ),
        name="block_sparse_product",
    )(slab, green.T, mask_slab, mask_green)
    return product.T


def solution(mesh):
    in_specs = (
        P(("layer", "row"), "col"),
        P(("layer", "col"), "row"),
        P(("layer", "row"), "col"),
        P(("layer", "col"), "row"),
    )
    out_specs = P("col", ("row", "layer"))
    return jax.shard_map(shards, mesh=mesh, in_specs=in_specs, out_specs=out_specs, check_vma=False)
```

time: 92.5 us -> 80.4 us (0.87)
  Pallas kernels: 90.4 us -> 76.3 us
  local copies, waits for them, and re-layouts: 1.95 us -> 3.89 us
    pallas_call x1, Pallas kernels: 90.4 us -> 76.3 us  [shards(): pl.pallas_call(kernel, out_shape=jax.ShapeDtypeStruct((6 * BLK, MB * BLK)...]
    unnamed x7 -> x9, local copies, waits for them, and re-layouts: 1.12 us -> 3.89 us
where the time goes in v2:
time: 80.4 us; the launch traced here: 80.2 us
  Pallas kernels  76.3 us (95%)
  local copies, waits for them, and re-layouts  3.89 us (5%)
    pallas_call x1, Pallas kernels, shards(): pl.pallas_call(kernel, out_shape=jax.ShapeDtypeStruct((6 * BLK, MB * BLK)...  76.3 us
    unnamed x9, local copies, waits for them, and re-layouts  3.89 us

profile of v2, /device:TPU:1, one launch (start us, length us, event | category | flops | bytes accessed | tf_op | source)
XLA Modules:
  0.0 80.2 jit_solution(7963511742388001444)
XLA Ops:
  0.0 0.0 copy-start
  0.0 0.9 %copy-done = bf16[115,736]{1,0:T(8,128)(2,1)S(1)} copy-done((bf16[115,736]{1,0:T(8,128)(2,1)S(1)}, bf16[115,736]{1,0:T(8,128)(2,1)}, u32[]{:S(2)}) %copy-start) | copy-done | bytes 169304
  0.9 0.0 copy-start.1
  0.9 0.9 %copy-done.1 = bf16[115,552]{0,1:T(8,128)(2,1)S(1)} copy-done((bf16[115,552]{0,1:T(8,128)(2,1)S(1)}, bf16[115,552]{0,1:T(8,128)(2,1)}, u32[]{:S(2)}) %copy-start.1) | copy-done | bytes 126984
  1.8 0.0 copy-start.2
  1.8 0.7 copy-done.2
  2.5 0.0 copy-start.3
  2.5 0.7 copy-done.3
  3.2 76.3 %block_sparse_product.1 = bf16[138,736]{1,0:T(8,128)(2,1)S(1)} custom-call(bf16[115,736]{1,0:T(8,128)(2,1)S(1)} %copy-done, bf16[552,115]{1,0:T(8,128)(2,1)S(1)} %bitcast.3, s32[5,32]{1,0:T(8,128)S(1)} %copy-done.2, s32[5,24]{1,0:T(8,128)S(1)} %copy-done.3), custom_call_target="tpu_custom_call" | custom-call | tf_op jit(solution)/shard_map/block_sparse_product/pallas_call | solution.py:387
  79.5 0.7 copy.6
Async XLA Ops:
  0.0 0.9 %copy-start = (bf16[115,736]{1,0:T(8,128)(2,1)S(1)}, bf16[115,736]{1,0:T(8,128)(2,1)}, u32[]{:S(2)}) copy-start(bf16[115,736]{1,0:T(8,128)(2,1)} %slab.1) | copy-start | bytes 507844
  0.9 0.9 %copy-start.1 = (bf16[115,552]{0,1:T(8,128)(2,1)S(1)}, bf16[115,552]{0,1:T(8,128)(2,1)}, u32[]{:S(2)}) copy-start(bf16[115,552]{0,1:T(8,128)(2,1)} %param.5) | copy-start | bytes 380884
  1.8 0.7 copy-start.2
  2.5 0.7 copy-start.3

commit v3 on v2

--- a/solution.py
+++ b/solution.py
@@ -69,10 +69,10 @@
     for tile in range(tiles):
         i = per * tile + inner
         source = jnp.where((code >= 0) & (i < BLK), block * BLK + i, -1)
-        rows_ref[pl.ds(0, KB * BLK), :] = dot(piece, one_hot(row == source), ((along,), (0,)))
+        rows_ref[tile, pl.ds(0, KB * BLK), :] = dot(piece, one_hot(row == source), ((along,), (0,)))
         packed = jnp.zeros((PITCH, 128), F32)
         for q in range(KB):
-            part = rows_ref[pl.ds(BLK * q, PITCH), :]
+            part = rows_ref[tile, pl.ds(BLK * q, PITCH), :]
             packed = packed + jnp.where(kb == q, part, 0.0)
         out.append(jnp.where(last, code.astype(F32), packed))
     return jnp.concatenate(out, axis=1)
@@ -137,8 +137,9 @@
 
 
 def kernel(
-    slab, green, mask_slab, mask_green, out,
-    sbuf, gbuf, relay, slab_all, green_all, acc, other, rows_ref, order,
+    slab_hbm, green_hbm, mask_slab_hbm, mask_green_hbm, out,
+    sbuf, gbuf, relay, slab_all, green_all, acc, other, green_rows, slab_rows, order,
+    slab, green, mask_slab, mask_green, in_sems,
     chain_send, near_send, ring_recv, hop_send, relay_recv, far_recv, xy_send, xy_recv, pair_sems,
 ):
     grid_row, zlo, layer = (lax.axis_index(a) for a in ("row", "col", "layer"))
@@ -157,6 +158,15 @@
     beside_y = [device(x, (y + d) % NY, z, core) for d in (1, 3, 2)]
     sibling = device(x, y, z, 1 - core)
     hops = (8, -8)
+
+    loads = [
+        pltpu.make_async_copy(src, dst, in_sems.at[i])
+        for i, (src, dst) in enumerate(
+            [(mask_green_hbm, mask_green), (green_hbm, green), (mask_slab_hbm, mask_slab), (slab_hbm, slab)]
+        )
+    ]
+    for load in loads:
+        load.start()
 
     barrier = pltpu.get_barrier_semaphore()
     partners = [*(along(d) for d in (1, -1, 3, -3, 8, -8)), *beside_x, *beside_y, sibling]
@@ -238,35 +248,47 @@
                 slab_arrived(which, ((x + q) % NX) * NY + (y + d) % NY, 0)
                 slab_arrived(which, ((x + d) % NX) * NY + (y + q) % NY, 1)
 
-    def take_slab(which, row):
-        upper = sbuf[which, row, 0].astype(F32)
-        lower = sbuf[which, row, 1].astype(F32)
-        packet = jnp.concatenate([upper[:PITCH], upper[PITCH:], lower[:PITCH], lower[PITCH:]], axis=1)
-        at = pl.multiple_of((which * 16 + row) * 128, 128)
-        slab_all[pl.ds(at, 128), :] = unpack_slab(packet)
-
-    def take_green(off):
-        slot = slot_at(off)
-        both = gbuf[slot].astype(F32)
-        packet = jnp.concatenate([both[:PITCH], both[PITCH:]], axis=1)
-        at = pl.multiple_of(slot * 128, 128)
-        green_all[pl.ds(at, 128), :] = unpack_green(packet, hi)
-
-    def multiply(part):
-        at = pl.multiple_of(part * 512, 512)
-        left = slab_all[pl.ds(at, 512), :]
-        for g in range(3):
-            term = dot(green_all[pl.ds(at, 512), 128 * g : 128 * g + 128], left, ((0,), (0,)))
-            acc[0, 64 * g : 64 * g + 64, :] += term[:64]
-            acc[1, 64 * g : 64 * g + 64, :] += term[64:]
+    def take_slabs(which, first):
+        done = []
+        for row in range(4):
+            upper = sbuf[which, first + row, 0].astype(F32)
+            lower = sbuf[which, first + row, 1].astype(F32)
+            done.append(unpack_slab(
+                jnp.concatenate([upper[:PITCH], upper[PITCH:], lower[:PITCH], lower[PITCH:]], axis=1)
+            ))
+        at = pl.multiple_of((which * 16 + first) * 128, 512)
+        slab_all[pl.ds(at, 512), :] = jnp.concatenate(done, axis=0)
+
+    def take_greens(offs):
+        slots = [slot_at(off) for off in offs]
+        done = []
+        for slot in slots:
+            both = gbuf[slot].astype(F32)
+            done.append(unpack_green(jnp.concatenate([both[:PITCH], both[PITCH:]], axis=1), hi))
+        for slot, rows in zip(slots, done):
+            green_all[pl.ds(pl.multiple_of(slot * 128, 128), 128), :] = rows
+
+    def product(which, tile):
+        at = pl.multiple_of(which * 2048, 2048)
+        left = slab_all[pl.ds(at, 2048), 256 * tile : 256 * tile + 256]
+        return dot(green_all[pl.ds(at, 2048), :], left, ((0,), (0,)))
+
+    def swap(tile):
+        part = acc.at[1 - core, :, pl.ds(256 * tile, 256)]
+        return copy(part, other.at[:, pl.ds(256 * tile, 256)], pair_sems.at[0, tile], pair_sems.at[1, tile], sibling)
 
     def loop(start, stop, body):
         lax.fori_loop(start, stop, lambda i, carry: (body(i), carry)[1], 0)
 
-    rows_ref[...] = jnp.zeros_like(rows_ref)
-    packet = pack(green[...], mask_green[...], NB, GREEN_SLOTS, GREEN_PER, GREEN_TILES, rows_ref, 0)
+    for rows in (green_rows, slab_rows):
+        rows[...] = jnp.zeros_like(rows)
+    loads[0].wait()
+    loads[1].wait()
+    packet = pack(green[...], mask_green[...], NB, GREEN_SLOTS, GREEN_PER, GREEN_TILES, green_rows, 0)
     gbuf[z] = jnp.concatenate([packet[:, :384], packet[:, 384:]], axis=0).astype(BF16)
-    packet = pack(slab[...], mask_slab[...], MB, SLAB_SLOTS, SLAB_PER, SLAB_TILES, rows_ref, 1)
+    loads[2].wait()
+    loads[3].wait()
+    packet = pack(slab[...], mask_slab[...], MB, SLAB_SLOTS, SLAB_PER, SLAB_TILES, slab_rows, 1)
     for side in range(2):
         quarters = [packet[:, 512 * side + 256 * g : 512 * side + 256 * g + 256] for g in range(2)]
         sbuf[hi, grid_row, side] = jnp.concatenate(quarters, axis=0).astype(BF16)
@@ -279,8 +301,7 @@
     near(0, 0, -1).start()
     start_first(hi)
     order[...] = columns_back()
-    acc[...] = jnp.zeros_like(acc)
-    take_green(0)
+    take_greens([0])
 
     def advance(step):
         green_arrived(-3 * step)
@@ -321,45 +342,47 @@
         def _():
             start_second(away)
 
-        take_green(-3 * step)
-        take_green(3 * step)
         before = 3 * (step - 1)
         green_arrived(-before - 1)
-        take_green(-before - 1)
         green_arrived(before + 1)
-        take_green(before + 1)
 
         @pl.when(step > 1)
         def _():
             green_arrived(1 - before)
-            take_green(1 - before)
             green_arrived(before - 1)
-            take_green(before - 1)
+
+        take_greens([-3 * step, 3 * step, -before - 1, before + 1, 1 - before, before - 1])
 
         @pl.when(step == 3)
         def _():
-            loop(0, 6, lambda row: take_slab(hi, row))
-
-        @pl.when(step == 4)
-        def _():
-            loop(6, 11, lambda row: take_slab(hi, row))
-
-        @pl.when(step == 5)
-        def _():
-            loop(11, 16, lambda row: take_slab(hi, row))
+            take_slabs(hi, 0)
+
+        @pl.when(step > 3)
+        def _():
+            take_slabs(hi, 4 * (step - 3))
 
     loop(1, 6, advance)
+    take_slabs(hi, 12)
     for off in (-16, -14, 14):
         green_arrived(off)
-        take_green(off)
-    loop(0, 4, lambda part: multiply(4 * hi + part))
+    take_greens([-16, -14, 14])
+    for tile in range(3):
+        term = product(hi, tile)
+        for g in range(3):
+            for c in range(2):
+                at = 128 * g + 64 * c
+                acc[c, 64 * g : 64 * g + 64, 256 * tile : 256 * tile + 256] = term[at : at + 64]
     wait_second(away)
-    loop(0, 16, lambda row: take_slab(away, row))
-    loop(0, 4, lambda part: multiply(4 * away + part))
-
-    swap = copy(acc.at[1 - core], other, pair_sems.at[0], pair_sems.at[1], sibling)
-    swap.start()
-    swap.wait()
+    loop(0, 4, lambda part: take_slabs(away, 4 * part))
+    for tile in range(3):
+        term = product(away, tile)
+        for g in range(3):
+            for c in range(2):
+                at = 128 * g + 64 * c
+                acc[c, 64 * g : 64 * g + 64, 256 * tile : 256 * tile + 256] += term[at : at + 64]
+        swap(tile).start()
+    for tile in range(3):
+        swap(tile).wait()
     out[...] = put_back((acc[core] + other[...]).astype(BF16), order[...])
 
     for way in range(2):
@@ -387,7 +410,7 @@
     product = pl.pallas_call(
         kernel,
         out_shape=jax.ShapeDtypeStruct((6 * BLK, MB * BLK), BF16),
-        in_specs=[vmem] * 4,
+        in_specs=[pl.BlockSpec(memory_space=pl.ANY)] * 4,
         out_specs=vmem,
         scratch_shapes=[
             pltpu.VMEM((2, 16, 2, 2 * PITCH, 256), BF16),
@@ -397,8 +420,14 @@
             pltpu.VMEM((32 * 128, 384), BF16),
             pltpu.VMEM((2, 192, 768), F32),
             pltpu.VMEM((192, 768), F32),
-            pltpu.VMEM((120, 128), F32),
+            pltpu.VMEM((GREEN_TILES, 120, 128), F32),
+            pltpu.VMEM((SLAB_TILES, 120, 128), F32),
             pltpu.VMEM((768, MB * BLK), BF16),
+            pltpu.VMEM((KB * BLK, MB * BLK), BF16),
+            pltpu.VMEM((NB * BLK, KB * BLK), BF16),
+            pltpu.VMEM((KB, MB), jnp.int32),
+            pltpu.VMEM((KB, NB), jnp.int32),
+            dma((4,)),
             dma((2, 5)),
             dma((2, 6, 2)),
             dma((NZ,)),
@@ -407,10 +436,10 @@
             dma((2,)),
             dma((2, 2, 5, 3)),
             dma((2, 16, 2)),
-            dma((2,)),
+            dma((2, 3)),
         ],
         compiler_params=pltpu.CompilerParams(
-            collective_id=0, has_side_effects=True, vmem_limit_bytes=48 * 1024 * 1024
+            collective_id=0, has_side_effects=True, vmem_limit_bytes=60 * 1024 * 1024
         ),
         name="block_sparse_product",
     )(slab, green.T, mask_slab, mask_green)

time: 80.4 us -> 74.4 us (0.925)
  Pallas kernels: 76.3 us -> 72.6 us
  local copies, waits for them, and re-layouts: 3.89 us -> 1.64 us
    pallas_call x1, Pallas kernels: 76.3 us -> 72.6 us  [shards(): pl.pallas_call(kernel, out_shape=jax.ShapeDtypeStruct((6 * BLK, MB * BLK)...]
    unnamed x9 -> x1, local copies, waits for them, and re-layouts: 3.89 us -> 1.64 us
where the time goes in v3:
time: 74.4 us; the launch traced here: 74.2 us
  Pallas kernels  72.6 us (98%)
  local copies, waits for them, and re-layouts  1.64 us (2%)
    pallas_call x1, Pallas kernels, shards(): pl.pallas_call(kernel, out_shape=jax.ShapeDtypeStruct((6 * BLK, MB * BLK)...  72.6 us
    unnamed x1, local copies, waits for them, and re-layouts  1.64 us

profile of v3, /device:TPU:1, one launch (start us, length us, event | category | flops | bytes accessed | tf_op | source)
XLA Modules:
  0.0 74.2 jit_solution(4140522337313680206)
XLA Ops:
  0.0 72.6 %block_sparse_product.1 = bf16[138,736]{1,0:T(8,128)(2,1)} custom-call(bf16[115,736]{1,0:T(8,128)(2,1)} %slab_hbm.1, bf16[552,115]{1,0:T(8,128)(2,1)} %bitcast.3, s32[5,32]{1,0:T(8,128)} %mask_slab_hbm.1, s32[5,24]{1,0:T(8,128)} %mask_green_hbm.1), custom_call_target="tpu_custom_call" | custom-call | tf_op jit(solution)/shard_map/block_sparse_product/pallas_call | solution.py:410
  72.6 1.6 %copy.6 = bf16[736,138]{0,1:T(8,128)(2,1)} copy(bf16[736,138]{0,1:T(8,128)(2,1)} %bitcast.2) | data formatting | bytes 406272

commit v4 on v3

--- a/solution.py
+++ b/solution.py
@@ -242,22 +242,34 @@
                 for c in second_phase(which, q, d):
                     c.start()
 
-    def wait_second(which):
-        for q in range(4):
-            for d in (1, 2, 3):
-                slab_arrived(which, ((x + q) % NX) * NY + (y + d) % NY, 0)
-                slab_arrived(which, ((x + d) % NX) * NY + (y + q) % NY, 1)
-
-    def take_slabs(which, first):
+    def row_at(dx, dy):
+        return ((x + dx) % NX) * NY + (y + dy) % NY
+
+    def take_second(which, group):
+        for dx, dy in group:
+            if dy:
+                slab_arrived(which, row_at(dx, dy), 0)
+            if dx:
+                slab_arrived(which, row_at(dx, dy), 1)
+        take_slabs(which, [row_at(dx, dy) for dx, dy in group])
+
+    groups = [
+        [(0, 0), (0, 3), (3, 0), (3, 3)],
+        [(0, 1), (1, 0), (1, 1), (3, 1)],
+        [(1, 3), (0, 2), (2, 0), (3, 2)],
+        [(2, 3), (1, 2), (2, 1), (2, 2)],
+    ]
+
+    def take_slabs(which, rows):
         done = []
-        for row in range(4):
-            upper = sbuf[which, first + row, 0].astype(F32)
-            lower = sbuf[which, first + row, 1].astype(F32)
+        for row in rows:
+            upper = sbuf[which, row, 0].astype(F32)
+            lower = sbuf[which, row, 1].astype(F32)
             done.append(unpack_slab(
                 jnp.concatenate([upper[:PITCH], upper[PITCH:], lower[:PITCH], lower[PITCH:]], axis=1)
             ))
-        at = pl.multiple_of((which * 16 + first) * 128, 512)
-        slab_all[pl.ds(at, 512), :] = jnp.concatenate(done, axis=0)
+        for row, values in zip(rows, done):
+            slab_all[pl.ds(pl.multiple_of((which * 16 + row) * 128, 128), 128), :] = values
 
     def take_greens(offs):
         slots = [slot_at(off) for off in offs]
@@ -268,10 +280,8 @@
         for slot, rows in zip(slots, done):
             green_all[pl.ds(pl.multiple_of(slot * 128, 128), 128), :] = rows
 
-    def product(which, tile):
-        at = pl.multiple_of(which * 2048, 2048)
-        left = slab_all[pl.ds(at, 2048), 256 * tile : 256 * tile + 256]
-        return dot(green_all[pl.ds(at, 2048), :], left, ((0,), (0,)))
+    def product(tile):
+        return dot(green_all[...], slab_all[:, 256 * tile : 256 * tile + 256], ((0,), (0,)))
 
     def swap(tile):
         part = acc.at[1 - core, :, pl.ds(256 * tile, 256)]
@@ -325,7 +335,28 @@
         def _():
             start_second(hi)
 
-        @pl.when(step == 2)
+        @pl.when(step == 3)
+        def _():
+            for side in range(2):
+                second_hop(side).wait_recv()
+            start_first(away)
+
+        @pl.when(step == 4)
+        def _():
+            start_second(away)
+
+        before = 3 * (step - 1)
+        green_arrived(-before - 1)
+        green_arrived(before + 1)
+
+        @pl.when(step > 1)
+        def _():
+            green_arrived(1 - before)
+            green_arrived(before - 1)
+
+        take_greens([-3 * step, 3 * step, -before - 1, before + 1, 1 - before, before - 1])
+
+        @pl.when(step == 1)
         def _():
             for side in range(2):
                 first_hop(side).wait_recv()
@@ -333,53 +364,29 @@
 
         @pl.when(step == 3)
         def _():
-            for side in range(2):
-                second_hop(side).wait_recv()
-            start_first(away)
-            wait_second(hi)
+            take_second(hi, groups[0])
 
         @pl.when(step == 4)
         def _():
-            start_second(away)
-
-        before = 3 * (step - 1)
-        green_arrived(-before - 1)
-        green_arrived(before + 1)
-
-        @pl.when(step > 1)
-        def _():
-            green_arrived(1 - before)
-            green_arrived(before - 1)
-
-        take_greens([-3 * step, 3 * step, -before - 1, before + 1, 1 - before, before - 1])
-
-        @pl.when(step == 3)
-        def _():
-            take_slabs(hi, 0)
-
-        @pl.when(step > 3)
-        def _():
-            take_slabs(hi, 4 * (step - 3))
+            take_second(hi, groups[1])
+
+        @pl.when(step == 5)
+        def _():
+            take_second(hi, groups[2])
 
     loop(1, 6, advance)
-    take_slabs(hi, 12)
+    take_second(hi, groups[3])
+    for group in groups:
+        take_second(away, group)
     for off in (-16, -14, 14):
         green_arrived(off)
     take_greens([-16, -14, 14])
     for tile in range(3):
-        term = product(hi, tile)
+        term = product(tile)
         for g in range(3):
             for c in range(2):
                 at = 128 * g + 64 * c
                 acc[c, 64 * g : 64 * g + 64, 256 * tile : 256 * tile + 256] = term[at : at + 64]
-    wait_second(away)
-    loop(0, 4, lambda part: take_slabs(away, 4 * part))
-    for tile in range(3):
-        term = product(away, tile)
-        for g in range(3):
-            for c in range(2):
-                at = 128 * g + 64 * c
-                acc[c, 64 * g : 64 * g + 64, 256 * tile : 256 * tile + 256] += term[at : at + 64]
         swap(tile).start()
     for tile in range(3):
         swap(tile).wait()

time: 74.4 us -> 72.1 us (0.969)
  Pallas kernels: 72.6 us -> 70.3 us
    pallas_call x1, Pallas kernels: 72.6 us -> 70.3 us  [shards(): pl.pallas_call(kernel, out_shape=jax.ShapeDtypeStruct((6 * BLK, MB * BLK)...]
where the time goes in v4:
time: 72.1 us; the launch traced here: 71.9 us
  Pallas kernels  70.3 us (98%)
  local copies, waits for them, and re-layouts  1.64 us (2%)
    pallas_call x1, Pallas kernels, shards(): pl.pallas_call(kernel, out_shape=jax.ShapeDtypeStruct((6 * BLK, MB * BLK)...  70.3 us
    unnamed x1, local copies, waits for them, and re-layouts  1.64 us

profile of v4, /device:TPU:1, one launch (start us, length us, event | category | flops | bytes accessed | tf_op | source)
XLA Modules:
  0.0 71.9 jit_solution(176402804445572701)
XLA Ops:
  0.0 70.3 %block_sparse_product.1 = bf16[138,736]{1,0:T(8,128)(2,1)} custom-call(bf16[115,736]{1,0:T(8,128)(2,1)} %slab_hbm.1, bf16[552,115]{1,0:T(8,128)(2,1)} %bitcast.3, s32[5,32]{1,0:T(8,128)} %mask_slab_hbm.1, s32[5,24]{1,0:T(8,128)} %mask_green_hbm.1), custom_call_target="tpu_custom_call" | custom-call | tf_op jit(solution)/shard_map/block_sparse_product/pallas_call | solution.py:417
  70.3 1.6 %copy.6 = bf16[736,138]{0,1:T(8,128)(2,1)} copy(bf16[736,138]{0,1:T(8,128)(2,1)} %bitcast.2) | data formatting | bytes 406272
